TPU v7x, 128 devices: a whole 4x4x4 slice. The times are simulated.
128 devices in a mesh: dp: 8 (over x, core), expert: 16 (over z, y).
Axes of the slice: x: 4, y: 4, z: 4, core: 2. Of those that a mesh axis runs over, the one named last changes fastest.
Arguments:
- coded: bfloat16 [16384, 2048], P(('dp', 'expert')), may hold values from -6 to 6
- block_scale: float32 [16384, 16], P(('dp', 'expert')), may hold values from 0.25 to 4
- routes: int32 [16384, 2], P(('dp', 'expert')), may hold values from 0 to 63, all different within a row; in each aligned block of 128 rows (0 to 127, 128 to 255, ...) at most 8 rows name the same one
- route_weight: float32 [16384, 2], P(('dp', 'expert')), may hold values from 0.2 to 1
- cotangent: bfloat16 [16384, 2048], P(('dp', 'expert')), may hold values from -6 to 6
- w_gate: bfloat16 [128, 2048, 704], P(('dp', 'expert')), may hold values from -0.125 to 0.125
- w_up: bfloat16 [128, 2048, 704], P(('dp', 'expert')), may hold values from -0.125 to 0.125
- w_down: bfloat16 [128, 704, 2048], P(('dp', 'expert')), may hold values from -0.15625 to 0.15625
Outputs:
- layer_out: bfloat16 [16384, 2048], P(('dp', 'expert'))
- grad_input: bfloat16 [16384, 2048], P(('dp', 'expert'))
- grad_weight: float32 [16384, 2], P(('dp', 'expert'))
- grad_gate: bfloat16 [128, 2048, 704], P(('dp', 'expert'))
- grad_up: bfloat16 [128, 2048, 704], P(('dp', 'expert'))
- grad_down: bfloat16 [128, 704, 2048], P(('dp', 'expert'))
Inputs may be any that keep to these rules, and one draw needn't show every extreme that they name: The two experts of a token differ. Among the routes of the tokens of one device (aligned blocks of 128 tokens) at most 8 name one expert, and some block of every draw has exactly 8 routes to one expert.
All inputs are finite; a program needn't handle non-finite values.
Results may differ from a plain program's by a relative error of at most 0.0079.
Values may be sent and summed in bfloat16 or wider, within the bound.
No kernel may reach another device: no remote copies, remote signals or barrier semaphores. Data moves between devices by JAX's collectives and lax.ppermute only.
A program may use at most 128 MiB of HBM per device.

v0:
```python
import jax
import jax.numpy as jnp
from jax import lax
from jax.experimental import pallas as pl
from jax.experimental.pallas import tpu as pltpu
from jax.sharding import PartitionSpec as P

AXES = ("dp", "expert")
CAP = 8
VMEM_LIMIT = 48 * 1024 * 1024


def row_to_column(row, size):
    eye = lax.broadcasted_iota(jnp.int32, (size, size), 0) == lax.broadcasted_iota(jnp.int32, (size, size), 1)
    return jnp.sum(jnp.where(eye, row, 0.0), axis=1, keepdims=True)


def column_to_row(column, size):
    eye = lax.broadcasted_iota(jnp.int32, (size, size), 0) == lax.broadcasted_iota(jnp.int32, (size, size), 1)
    return jnp.sum(jnp.where(eye, column, 0.0), axis=0, keepdims=True)


def plan_kernel(experts, tokens, routes_ref, weight_ref, pick_ref, slot_weight_ref, position_ref):
    numbers = lax.broadcasted_iota(jnp.int32, (experts, tokens), 0)
    first = routes_ref[0:1, :] == numbers
    second = routes_ref[1:2, :] == numbers
    named = jnp.where(first | second, 1.0, 0.0)
    earlier = lax.broadcasted_iota(jnp.int32, (tokens, tokens), 0) < lax.broadcasted_iota(jnp.int32, (tokens, tokens), 1)
    rank = jnp.dot(
        named.astype(jnp.bfloat16),
        jnp.where(earlier, 1.0, 0.0).astype(jnp.bfloat16),
        preferred_element_type=jnp.float32,
    )
    weight = jnp.where(first, weight_ref[0:1, :], 0.0) + jnp.where(second, weight_ref[1:2, :], 0.0)
    slots = lax.broadcasted_iota(jnp.int32, (experts, CAP, tokens), 1).astype(jnp.float32)
    slot_of = jnp.where(named > 0.0, rank, -1.0)
    pick = jnp.broadcast_to(slot_of[:, None, :], (experts, CAP, tokens)) == slots
    pick_ref[...] = jnp.where(pick, 1.0, 0.0).astype(jnp.bfloat16).reshape(experts * CAP, tokens)
    spread = jnp.broadcast_to(weight[:, None, :], (experts, CAP, tokens))
    slot_weight_ref[...] = jnp.sum(jnp.where(pick, spread, 0.0).reshape(experts * CAP, tokens), axis=1, keepdims=True)
    place = numbers.astype(jnp.float32) * CAP + rank
    position_ref[0:1, :] = jnp.sum(jnp.where(first, place, 0.0), axis=0, keepdims=True).astype(jnp.int32)
    position_ref[1:2, :] = jnp.sum(jnp.where(second, place, 0.0), axis=0, keepdims=True).astype(jnp.int32)


def plan(routes, weight):
    tokens = routes.shape[1]
    experts = tokens // 2
    return pl.pallas_call(
        lambda *refs: plan_kernel(experts, tokens, *refs),
        out_shape=(
            jax.ShapeDtypeStruct((experts * CAP, tokens), jnp.bfloat16),
            jax.ShapeDtypeStruct((experts * CAP, 1), jnp.float32),
            jax.ShapeDtypeStruct((2, tokens), jnp.int32),
        ),
        name="plan",
    )(routes, weight)


def send_in_kernel(coded_ref, scale_ref, pick_ref, out_ref, inputs_ref):
    tokens, width = coded_ref.shape
    blocks = scale_ref.shape[0]
    size = width // blocks

    @pl.when(pl.program_id(0) == 0)
    def _():
        for b in range(blocks):
            columns = pl.ds(b * size, size)
            scale = row_to_column(scale_ref[b : b + 1, :], tokens)
            inputs_ref[:, columns] = (coded_ref[:, columns].astype(jnp.float32) * scale).astype(jnp.bfloat16)

    rows = jnp.dot(pick_ref[...], inputs_ref[...], preferred_element_type=jnp.float32).astype(jnp.bfloat16)
    rows = rows.reshape(-1, CAP, width)
    out_ref[:, 0] = rows
    out_ref[:, 1] = rows


def send_in(coded, scale, pick, steps=4):
    tokens, width = coded.shape
    experts = pick.shape[0] // CAP
    return pl.pallas_call(
        send_in_kernel,
        grid=(steps,),
        in_specs=[
            pl.BlockSpec(coded.shape, lambda i: (0, 0)),
            pl.BlockSpec(scale.shape, lambda i: (0, 0)),
            pl.BlockSpec((experts * CAP // steps, tokens), lambda i: (i, 0)),
        ],
        out_specs=pl.BlockSpec((experts // steps, 2, CAP, width), lambda i: (i, 0, 0, 0)),
        out_shape=jax.ShapeDtypeStruct((experts, 2, CAP, width), jnp.bfloat16),
        scratch_shapes=[pltpu.VMEM((tokens, width), jnp.bfloat16)],
        compiler_params=pltpu.CompilerParams(vmem_limit_bytes=VMEM_LIMIT),
        name="send_in",
    )(coded, scale, pick)


def send_cot_kernel(cot_ref, pick_ref, weight_ref, out_ref):
    rows = jnp.dot(pick_ref[...], cot_ref[...], preferred_element_type=jnp.float32)
    rows = (rows * weight_ref[...]).astype(jnp.bfloat16).reshape(-1, CAP, cot_ref.shape[1])
    out_ref[:, 0] = rows
    out_ref[:, 1] = rows


def send_cot(cotangent, pick, slot_weight, steps=4):
    tokens, width = cotangent.shape
    experts = pick.shape[0] // CAP
    return pl.pallas_call(
        send_cot_kernel,
        grid=(steps,),
        in_specs=[
            pl.BlockSpec(cotangent.shape, lambda i: (0, 0)),
            pl.BlockSpec((experts * CAP // steps, tokens), lambda i: (i, 0)),
            pl.BlockSpec((experts * CAP // steps, 1), lambda i: (i, 0)),
        ],
        out_specs=pl.BlockSpec((experts // steps, 2, CAP, width), lambda i: (i, 0, 0, 0)),
        out_shape=jax.ShapeDtypeStruct((experts, 2, CAP, width), jnp.bfloat16),
        compiler_params=pltpu.CompilerParams(vmem_limit_bytes=VMEM_LIMIT),
        cost_estimate=pl.CostEstimate(flops=2 * experts * CAP * tokens * width, bytes_accessed=10_000_000, transcendentals=0),
        name="send_cot",
    )(cotangent, pick, slot_weight)


def pair_rows(back_ref):
    both = back_ref[:, 0].astype(jnp.float32) + back_ref[:, 1].astype(jnp.float32)
    experts, cap, width = both.shape
    return both.reshape(experts * cap, width).astype(jnp.bfloat16)


def gather_rows(position, rows):
    numbers = lax.broadcasted_iota(jnp.int32, (rows.shape[0], position.shape[1]), 0)
    hit = jnp.where(numbers == position, 1.0, 0.0).astype(jnp.bfloat16)
    return lax.dot_general(hit, rows, (((0,), (0,)), ((), ())), preferred_element_type=jnp.float32)


def finish_out_kernel(back_ref, position_ref, weight_ref, cot_ref, out_ref, grad_ref):
    tokens = position_ref.shape[1]
    rows = pair_rows(back_ref)
    first = gather_rows(position_ref[0:1, :], rows)
    second = gather_rows(position_ref[1:2, :], rows)
    cot = cot_ref[...].astype(jnp.float32)
    total = first * row_to_column(weight_ref[0:1, :], tokens) + second * row_to_column(weight_ref[1:2, :], tokens)
    out_ref[...] = total.astype(jnp.bfloat16)

    @pl.when(pl.program_id(0) == 0)
    def _():
        grad_ref[...] = jnp.zeros_like(grad_ref)

    grad_ref[0:1, :] += column_to_row(jnp.sum(cot * first, axis=1, keepdims=True), tokens)
    grad_ref[1:2, :] += column_to_row(jnp.sum(cot * second, axis=1, keepdims=True), tokens)


def finish_out(back, position, weight, cotangent, steps=4):
    experts, _, cap, width = back.shape
    tokens = cotangent.shape[0]
    part = width // steps
    return pl.pallas_call(
        finish_out_kernel,
        grid=(steps,),
        in_specs=[
            pl.BlockSpec((experts, 2, cap, part), lambda i: (0, 0, 0, i)),
            pl.BlockSpec(position.shape, lambda i: (0, 0)),
            pl.BlockSpec(weight.shape, lambda i: (0, 0)),
            pl.BlockSpec((tokens, part), lambda i: (0, i)),
        ],
        out_specs=(
            pl.BlockSpec((tokens, part), lambda i: (0, i)),
            pl.BlockSpec((2, tokens), lambda i: (0, 0)),
        ),
        out_shape=(
            jax.ShapeDtypeStruct((tokens, width), jnp.bfloat16),
            jax.ShapeDtypeStruct((2, tokens), jnp.float32),
        ),
        compiler_params=pltpu.CompilerParams(vmem_limit_bytes=VMEM_LIMIT),
        cost_estimate=pl.CostEstimate(flops=4 * experts * cap * tokens * width, bytes_accessed=10_000_000, transcendentals=0),
        name="finish_out",
    )(back, position, weight, cotangent)


def finish_in_kernel(back_ref, position_ref, out_ref):
    rows = pair_rows(back_ref)
    total = gather_rows(position_ref[0:1, :], rows) + gather_rows(position_ref[1:2, :], rows)
    out_ref[...] = total.astype(jnp.bfloat16)


def finish_in(back, position, steps=4):
    experts, _, cap, width = back.shape
    tokens = position.shape[1]
    part = width // steps
    return pl.pallas_call(
        finish_in_kernel,
        grid=(steps,),
        in_specs=[
            pl.BlockSpec((experts, 2, cap, part), lambda i: (0, 0, 0, i)),
            pl.BlockSpec(position.shape, lambda i: (0, 0)),
        ],
        out_specs=pl.BlockSpec((tokens, part), lambda i: (0, i)),
        out_shape=jax.ShapeDtypeStruct((tokens, width), jnp.bfloat16),
        compiler_params=pltpu.CompilerParams(vmem_limit_bytes=VMEM_LIMIT),
        name="finish_in",
    )(back, position)


def dot(a, b, a_dim, b_dim):
    return lax.dot_general(a, b, (((a_dim,), (b_dim,)), ((), ())), preferred_element_type=jnp.float32)


def exchange(rows):
    return lax.all_to_all(rows, AXES, split_axis=0, concat_axis=0, tiled=True)


def on_device(coded, block_scale, routes, route_weight, cotangent, w_gate, w_up, w_down):
    tokens, width = coded.shape
    nodes = lax.axis_size(AXES)
    weight = route_weight.T
    gate_w, up_w, down_w = w_gate[0].T, w_up[0].T, w_down[0]

    pick, slot_weight, position = plan(routes.T, weight)
    rows = exchange(send_in(coded, block_scale.T, pick).reshape(nodes, CAP, width))
    cot_rows = exchange(send_cot(cotangent, pick, slot_weight).reshape(nodes, CAP, width))
    rows = rows.reshape(-1, width)
    cot_rows = cot_rows.reshape(-1, width)

    gate = dot(rows, gate_w, 1, 1)
    upper = dot(rows, up_w, 1, 1)
    sigma = jax.nn.sigmoid(gate)
    active = gate * sigma
    hidden = (active * upper).astype(jnp.bfloat16)
    partial_out = dot(hidden, down_w, 1, 0).astype(jnp.bfloat16)
    back_out = exchange(partial_out.reshape(nodes, CAP, width))

    d_hidden = dot(cot_rows, down_w, 1, 1)
    d_upper = (d_hidden * active).astype(jnp.bfloat16)
    d_gate = (d_hidden * upper * sigma * (1.0 + gate * (1.0 - sigma))).astype(jnp.bfloat16)
    partial_in = (dot(d_gate, gate_w, 1, 0) + dot(d_upper, up_w, 1, 0)).astype(jnp.bfloat16)
    back_in = exchange(partial_in.reshape(nodes, CAP, width))

    grad_down = dot(hidden, cot_rows, 0, 0).astype(jnp.bfloat16)
    grad_gate = dot(d_gate, rows, 0, 0).astype(jnp.bfloat16)
    grad_up = dot(d_upper, rows, 0, 0).astype(jnp.bfloat16)

    back_out = back_out.reshape(nodes // 2, 2, CAP, width)
    back_in = back_in.reshape(nodes // 2, 2, CAP, width)
    layer_out, grad_weight = finish_out(back_out, position, weight, cotangent)
    grad_input = finish_in(back_in, position)
    return (layer_out, grad_input, grad_weight.T, grad_gate.T[None], grad_up.T[None], grad_down[None])


def solution(mesh):
    rows = P(AXES, None)
    matrix = P(AXES, None, None)
    return jax.shard_map(
        on_device,
        mesh=mesh,
        in_specs=(rows, rows, rows, rows, rows, matrix, matrix, matrix),
        out_specs=(rows, rows, rows, matrix, matrix, matrix),
        check_vma=False,
    )
```

profile of v0, /device:TPU:7, one launch (start us, length us, event | category | flops | bytes accessed | tf_op | source)
XLA Modules:
  0.0 262.9 jit_solution(3287562395985230497)
XLA Ops:
  0.6 0.0 copy-start
  0.6 1.8 plan.1
  2.5 0.0 copy-start.5
  2.5 1.0 copy-done.5
  3.5 0.0 copy-start.6
  3.5 0.9 copy-done.6
  4.4 0.0 copy-start.9
  4.4 0.7 copy-done.9
  5.1 1.5 send_in.1
  6.7 0.0 copy-start.3
  6.7 2.0 copy-done.3
  8.7 0.0 copy-start.4
  8.7 0.0 copy-start.7
  8.7 11.2 %all-to-all-start = ((bf16[128,8,2048]{2,1,0:T(8,128)(2,1)}), bf16[128,8,2048]{2,1,0:T(8,128)(2,1)}, u32[]{:S(2)}, u32[]{:S(2)}) async-start(bf16[128,8,2048]{2,1,0:T(8,128)(2,1)} %bitcast.70), calls=%async_computation | async-start | bytes 8388608 | tf_op jit(solution)/shard_map/all_to_all | solution.py:208
  20.0 0.0 copy-done.4
  20.0 0.0 copy-done.7
  20.0 0.0 copy-start.8
  20.0 0.9 copy-done.8
  20.9 1.2 send_cot.1
  22.1 0.0 copy-start.2
  22.1 2.0 copy-done.2
  24.1 47.8 %all-to-all-done = bf16[128,8,2048]{2,1,0:T(8,128)(2,1)} async-done(((bf16[128,8,2048]{2,1,0:T(8,128)(2,1)}), bf16[128,8,2048]{2,1,0:T(8,128)(2,1)}, u32[]{:S(2)}, u32[]{:S(2)}) %all-to-all-start) | async-done | bytes 4194336 | tf_op jit(solution)/shard_map/all_to_all | solution.py:208
  71.9 5.2 %all-to-all-start.2 = ((bf16[128,8,2048]{2,1,0:T(8,128)(2,1)}), bf16[128,8,2048]{2,1,0:T(8,128)(2,1)}, u32[]{:S(2)}, u32[]{:S(2)}) async-start(bf16[128,8,2048]{2,1,0:T(8,128)(2,1)} %bitcast.69), calls=%async_computation.2 | async-start | bytes 8388608 | tf_op jit(solution)/shard_map/all_to_all | solution.py:208
  77.1 0.0 copy-start.12
  77.1 8.0 %fusion.9 = f32[1024,704]{0,1:T(8,128)} fusion(bf16[128,8,2048]{2,1,0:T(8,128)(2,1)} %all-to-all-done, bf16[1,2048,704]{1,2,0:T(8,128)(2,1)} %param.14), kind=kOutput, calls=%fused_computation.10 | convolution fusion | flops 2952790016 | bytes 9961472 | tf_op jit(solution)/shard_map/dot_general | solution.py:204
  85.1 0.0 copy-done.12
  85.1 6.9 %fusion.11 = f32[1024,704]{0,1:T(8,128)} fusion(bf16[128,8,2048]{2,1,0:T(8,128)(2,1)} %all-to-all-done, bf16[1,2048,704]{1,2,0:T(8,128)(2,1)S(1)} %copy-done.12), kind=kOutput, calls=%fused_computation.12 | convolution fusion | flops 2952790016 | bytes 9961472 | tf_op jit(solution)/shard_map/dot_general | solution.py:204
  92.0 37.0 %all-to-all-done.2 = bf16[128,8,2048]{2,1,0:T(8,128)(2,1)} async-done(((bf16[128,8,2048]{2,1,0:T(8,128)(2,1)}), bf16[128,8,2048]{2,1,0:T(8,128)(2,1)}, u32[]{:S(2)}, u32[]{:S(2)}) %all-to-all-start.2) | async-done | bytes 4194336 | tf_op jit(solution)/shard_map/all_to_all | solution.py:208
  129.0 0.0 copy-done
  129.0 8.6 %multiply_convert_fusion = (bf16[1024,704]{0,1:T(8,128)(2,1)}, bf16[1024,704]{0,1:T(8,128)(2,1)}, bf16[1024,704]{0,1:T(8,128)(2,1)S(1)}) fusion(f32[1024,704]{0,1:T(8,128)} %fusion.11, f32[1024,704]{0,1:T(8,128)} %fusion.9, bf16[1,704,2048]{2,1,0:T(8,128)(2,1)S(1)} %copy-done, bf16[128,8,2048]{2,1,0:T(8,128)(2,1)} %all-to-all-done.2), kind=kOutput, calls=%fused_computation.28 | convolution fusion | flops 2963603456 | bytes 17170432 | tf_op jit(solution)/shard_map/dot_general | solution.py:204
  137.6 0.0 copy-start.18
  137.6 1.1 copy-done.18
  138.7 5.1 %convert_bitcast_fusion = bf16[128,8,2048]{2,1,0:T(8,128)(2,1)} fusion(bf16[1024,704]{0,1:T(8,128)(2,1)S(1)} %get-tuple-element.18, bf16[1,704,2048]{2,1,0:T(8,128)(2,1)S(1)} %copy-done), kind=kOutput, calls=%fused_computation.14 | convolution fusion | flops 2954887168 | bytes 8519680 | tf_op jit(solution)/shard_map/dot_general | solution.py:204
  143.8 0.0 copy-start.13
  143.8 5.3 %all-to-all-start.1 = ((bf16[128,8,2048]{2,1,0:T(8,128)(2,1)}), bf16[128,8,2048]{2,1,0:T(8,128)(2,1)}, u32[]{:S(2)}, u32[]{:S(2)}) async-start(bf16[128,8,2048]{2,1,0:T(8,128)(2,1)} %convert_bitcast_fusion), calls=%async_computation.1 | async-start | bytes 8388608 | tf_op jit(solution)/shard_map/all_to_all | solution.py:208
  149.0 0.0 copy-done.13
  149.0 0.0 copy-start.14
  149.0 0.0 copy-start.16
  149.1 5.0 %fusion.35 = f32[1024,2048]{1,0:T(8,128)S(1)} fusion(bf16[1024,704]{0,1:T(8,128)(2,1)} %get-tuple-element.17, bf16[1,2048,704]{1,2,0:T(8,128)(2,1)S(1)} %copy-done.13), kind=kOutput, calls=%fused_computation.25 | convolution fusion | flops 2952790016 | bytes 12713984 | tf_op jit(solution)/shard_map/dot_general | solution.py:204
  154.1 0.0 copy-done.14
  154.1 0.0 copy-done.16
  154.1 5.4 %fusion = bf16[128,8,2048]{2,1,0:T(8,128)(2,1)} fusion(f32[1024,2048]{1,0:T(8,128)S(1)} %fusion.35, bf16[1024,704]{0,1:T(8,128)(2,1)S(1)} %copy-done.16, bf16[1,2048,704]{1,2,0:T(8,128)(2,1)S(1)} %copy-done.14), kind=kOutput, calls=%fused_computation.1 | convolution fusion | flops 2956984320 | bytes 16908288 | tf_op jit(solution)/shard_map/dot_general | solution.py:204
  159.5 0.0 copy-start.19
  159.5 41.5 %all-to-all-done.1 = bf16[128,8,2048]{2,1,0:T(8,128)(2,1)} async-done(((bf16[128,8,2048]{2,1,0:T(8,128)(2,1)}), bf16[128,8,2048]{2,1,0:T(8,128)(2,1)}, u32[]{:S(2)}, u32[]{:S(2)}) %all-to-all-start.1) | async-done | bytes 4194336 | tf_op jit(solution)/shard_map/all_to_all | solution.py:208
  201.0 5.2 %all-to-all-start.3 = ((bf16[128,8,2048]{2,1,0:T(8,128)(2,1)}), bf16[128,8,2048]{2,1,0:T(8,128)(2,1)}, u32[]{:S(2)}, u32[]{:S(2)}) async-start(bf16[128,8,2048]{2,1,0:T(8,128)(2,1)} %fusion), calls=%async_computation.3 | async-start | bytes 8388608 | tf_op jit(solution)/shard_map/all_to_all | solution.py:208
  206.2 0.0 copy-done.19
  206.2 0.0 copy-start.17
  206.3 6.7 %fusion.22 = bf16[1,704,2048]{2,1,0:T(8,128)(2,1)} fusion(bf16[1024,704]{0,1:T(8,128)(2,1)S(1)} %copy-done.19, bf16[128,8,2048]{2,1,0:T(8,128)(2,1)} %all-to-all-done.2), kind=kOutput, calls=%fused_computation.18 | convolution fusion | flops 2954231808 | bytes 8519680 | tf_op jit(solution)/shard_map/dot_general | solution.py:204
  213.0 0.0 copy-done.17
  213.0 0.0 copy-start.15
  213.0 6.7 %fusion.28 = bf16[1,2048,704]{1,2,0:T(8,128)(2,1)} fusion(bf16[1024,704]{0,1:T(8,128)(2,1)S(1)} %copy-done.17, bf16[128,8,2048]{2,1,0:T(8,128)(2,1)} %all-to-all-done), kind=kOutput, calls=%fused_computation.20 | convolution fusion | flops 2954231808 | bytes 8519680 | tf_op jit(solution)/shard_map/dot_general | solution.py:204
  219.7 0.0 copy-done.15
  219.7 0.0 copy-start.10
  219.7 0.0 copy-start.11
  219.7 6.6 %fusion.25 = bf16[1,2048,704]{1,2,0:T(8,128)(2,1)} fusion(bf16[1024,704]{0,1:T(8,128)(2,1)S(1)} %copy-done.15, bf16[128,8,2048]{2,1,0:T(8,128)(2,1)} %all-to-all-done), kind=kOutput, calls=%fused_computation.19 | convolution fusion | flops 2954231808 | bytes 8519680 | tf_op jit(solution)/shard_map/dot_general | solution.py:204
  226.4 0.0 copy-done.10
  226.4 0.0 copy-done.11
  226.4 0.0 copy-start.1
  226.4 5.0 %finish_out.1 = (bf16[128,2048]{1,0:T(8,128)(2,1)}, f32[2,128]{1,0:T(2,128)}) custom-call(bf16[64,2,8,2048]{3,2,1,0:T(8,128)(2,1)} %bitcast.9.back_ref, s32[2,128]{1,0:T(2,128)S(1)} %copy-done.10, f32[2,128]{1,0:T(2,128)S(1)} %bitcast.73, bf16[128,2048]{1,0:T(8,128)(2,1)S(1)} %copy-done.4), custom_call_target="tpu_custom_call" | custom-call | flops 536870912 | bytes 10000000 | tf_op jit(solution)/shard_map/finish_out/pallas_call | solution.py:156
  231.4 26.8 %all-to-all-done.3 = bf16[128,8,2048]{2,1,0:T(8,128)(2,1)} async-done(((bf16[128,8,2048]{2,1,0:T(8,128)(2,1)}), bf16[128,8,2048]{2,1,0:T(8,128)(2,1)}, u32[]{:S(2)}, u32[]{:S(2)}) %all-to-all-start.3) | async-done | bytes 4194336 | tf_op jit(solution)/shard_map/all_to_all | solution.py:208
  258.2 4.7 %finish_in.1 = bf16[128,2048]{1,0:T(8,128)(2,1)} custom-call(bf16[64,2,8,2048]{3,2,1,0:T(8,128)(2,1)} %bitcast.13.back_ref, s32[2,128]{1,0:T(2,128)S(1)} %copy-done.10), custom_call_target="tpu_custom_call" | custom-call | tf_op jit(solution)/shard_map/finish_in/pallas_call | solution.py:189
  262.9 0.0 copy-done.1
Async XLA Ops:
  0.6 128.4 %copy-start = (bf16[1,704,2048]{2,1,0:T(8,128)(2,1)S(1)}, bf16[1,704,2048]{2,1,0:T(8,128)(2,1)}, u32[]{:S(2)}) copy-start(bf16[1,704,2048]{2,1,0:T(8,128)(2,1)} %param.15) | copy-start | bytes 8650756
  2.5 1.0 copy-start.5
  3.5 0.9 copy-start.6
  4.4 0.7 copy-start.9
  6.7 2.0 copy-start.3
  8.7 11.2 %copy-start.4 = (bf16[128,2048]{1,0:T(8,128)(2,1)S(1)}, bf16[128,2048]{1,0:T(8,128)(2,1)}, u32[]{:S(2)}) copy-start(bf16[128,2048]{1,0:T(8,128)(2,1)} %cot_ref.3) | copy-start | bytes 1572868
  8.7 11.3 %copy-start.7 = (bf16[512,128]{1,0:T(8,128)(2,1)S(1)}, bf16[512,128]{1,0:T(8,128)(2,1)}, u32[]{:S(2)}) copy-start(bf16[512,128]{1,0:T(8,128)(2,1)} %get-tuple-element.11.pick_ref) | copy-start | bytes 393220
  8.7 63.2 %all-to-all-start = ((bf16[128,8,2048]{2,1,0:T(8,128)(2,1)}), bf16[128,8,2048]{2,1,0:T(8,128)(2,1)}, u32[]{:S(2)}, u32[]{:S(2)}) async-start(bf16[128,8,2048]{2,1,0:T(8,128)(2,1)} %bitcast.70), calls=%async_computation | async-start | bytes 8388608 | tf_op jit(solution)/shard_map/all_to_all | solution.py:208
  20.0 1.0 copy-start.8
  22.1 2.0 copy-start.2
  71.9 57.1 %all-to-all-start.2 = ((bf16[128,8,2048]{2,1,0:T(8,128)(2,1)}), bf16[128,8,2048]{2,1,0:T(8,128)(2,1)}, u32[]{:S(2)}, u32[]{:S(2)}) async-start(bf16[128,8,2048]{2,1,0:T(8,128)(2,1)} %bitcast.69), calls=%async_computation.2 | async-start | bytes 8388608 | tf_op jit(solution)/shard_map/all_to_all | solution.py:208
  77.1 8.0 %copy-start.12 = (bf16[1,2048,704]{1,2,0:T(8,128)(2,1)S(1)}, bf16[1,2048,704]{1,2,0:T(8,128)(2,1)}, u32[]{:S(2)}) copy-start(bf16[1,2048,704]{1,2,0:T(8,128)(2,1)} %param.13) | copy-start | bytes 8650756
  137.6 1.1 copy-start.18
  143.8 5.3 %copy-start.13 = (bf16[1,2048,704]{1,2,0:T(8,128)(2,1)S(1)}, bf16[1,2048,704]{1,2,0:T(8,128)(2,1)}, u32[]{:S(2)}) copy-start(bf16[1,2048,704]{1,2,0:T(8,128)(2,1)} %param.13) | copy-start | bytes 8650756
  143.8 57.3 %all-to-all-start.1 = ((bf16[128,8,2048]{2,1,0:T(8,128)(2,1)}), bf16[128,8,2048]{2,1,0:T(8,128)(2,1)}, u32[]{:S(2)}, u32[]{:S(2)}) async-start(bf16[128,8,2048]{2,1,0:T(8,128)(2,1)} %convert_bitcast_fusion), calls=%async_computation.1 | async-start | bytes 8388608 | tf_op jit(solution)/shard_map/all_to_all | solution.py:208
  149.0 5.1 %copy-start.14 = (bf16[1,2048,704]{1,2,0:T(8,128)(2,1)S(1)}, bf16[1,2048,704]{1,2,0:T(8,128)(2,1)}, u32[]{:S(2)}) copy-start(bf16[1,2048,704]{1,2,0:T(8,128)(2,1)} %param.14) | copy-start | bytes 8650756
  149.0 5.1 %copy-start.16 = (bf16[1024,704]{0,1:T(8,128)(2,1)S(1)}, bf16[1024,704]{0,1:T(8,128)(2,1)}, u32[]{:S(2)}) copy-start(bf16[1024,704]{0,1:T(8,128)(2,1)} %get-tuple-element.16) | copy-start | bytes 4325380
  159.5 46.7 %copy-start.19 = (bf16[1024,704]{0,1:T(8,128)(2,1)S(1)}, bf16[1024,704]{0,1:T(8,128)(2,1)}, u32[]{:S(2)}) copy-start(bf16[1024,704]{0,1:T(8,128)(2,1)} %copy-done.18) | copy-start | bytes 4325380
  201.0 57.1 %all-to-all-start.3 = ((bf16[128,8,2048]{2,1,0:T(8,128)(2,1)}), bf16[128,8,2048]{2,1,0:T(8,128)(2,1)}, u32[]{:S(2)}, u32[]{:S(2)}) async-start(bf16[128,8,2048]{2,1,0:T(8,128)(2,1)} %fusion), calls=%async_computation.3 | async-start | bytes 8388608 | tf_op jit(solution)/shard_map/all_to_all | solution.py:208
  206.2 6.8 %copy-start.17 = (bf16[1024,704]{0,1:T(8,128)(2,1)S(1)}, bf16[1024,704]{0,1:T(8,128)(2,1)}, u32[]{:S(2)}) copy-start(bf16[1024,704]{0,1:T(8,128)(2,1)} %get-tuple-element.16) | copy-start | bytes 4325380
  213.0 6.7 %copy-start.15 = (bf16[1024,704]{0,1:T(8,128)(2,1)S(1)}, bf16[1024,704]{0,1:T(8,128)(2,1)}, u32[]{:S(2)}) copy-start(bf16[1024,704]{0,1:T(8,128)(2,1)} %get-tuple-element.17) | copy-start | bytes 4325380
  219.7 6.6 %copy-start.10 = (s32[2,128]{1,0:T(2,128)S(1)}, s32[2,128]{1,0:T(2,128)}, u32[]{:S(2)}) copy-start(s32[2,128]{1,0:T(2,128)} %get-tuple-element.12.position_ref) | copy-start | bytes 3076
  219.7 6.6 %copy-start.11 = (f32[128,2]{0,1:T(2,128)S(1)}, f32[128,2]{0,1:T(2,128)}, u32[]{:S(2)}) copy-start(f32[128,2]{0,1:T(2,128)} %param.11) | copy-start | bytes 3076
  226.4 36.5 %copy-start.1 = (bf16[1,704,2048]{2,1,0:T(8,128)(2,1)S(1)}, bf16[1,704,2048]{2,1,0:T(8,128)(2,1)}, u32[]{:S(2)}) copy-start(bf16[1,704,2048]{2,1,0:T(8,128)(2,1)} %param.15) | copy-start | bytes 8650756
where the time goes:
time: 264 us; the launch traced here: 263 us
  waiting for transfers between devices  153 us (58%)
  matrix products  59.1 us (22%)
  starting transfers between devices  26.8 us (10%)
  Pallas kernels  14.3 us (5%)
  local copies, waits for them, and re-layouts  8.75 us (3%)
    all_to_all x4, waiting for transfers between devices, exchange(): return lax.all_to_all(rows, AXES, split_axis=0, concat_axis=0, tiled=True)  153 us
    dot_general x9, matrix products, dot(): lax.dot_general(a, b, (((a_dim,), (b_dim,)), ((), ())), preferred_element...  59.1 us
    all_to_all x4, starting transfers between devices, exchange(): return lax.all_to_all(rows, AXES, split_axis=0, concat_axis=0, tiled=True)  26.8 us
    unnamed x40, local copies, waits for them, and re-layouts  8.75 us
  transfers between devices with their start and end apart: 4, of which 4 were waited for; matrix products, arithmetic and copies ran while one was open for 17% of the time, Pallas kernels for 2%

commit v1 on v0

v1 whole, which is shorter than its diff:
```python
import jax
import jax.numpy as jnp
from jax import lax
from jax.experimental import pallas as pl
from jax.experimental.pallas import tpu as pltpu
from jax.sharding import PartitionSpec as P

AXES = ("dp", "expert")
CAP = 8
VMEM_LIMIT = 60 * 1024 * 1024


def row_to_column(row, size):
    eye = lax.broadcasted_iota(jnp.int32, (size, size), 0) == lax.broadcasted_iota(jnp.int32, (size, size), 1)
    return jnp.sum(jnp.where(eye, row, 0.0), axis=1, keepdims=True)


def column_to_row(column, size):
    eye = lax.broadcasted_iota(jnp.int32, (size, size), 0) == lax.broadcasted_iota(jnp.int32, (size, size), 1)
    return jnp.sum(jnp.where(eye, column, 0.0), axis=0, keepdims=True)


def prepare_kernel(coded_hbm, scale_ref, routes_ref, weight_ref, out_ref, pick_ref, slot_weight_ref, place_ref, coded_ref, inputs_ref, sem):
    tokens, width = coded_ref.shape
    blocks = scale_ref.shape[0]
    size = width // blocks
    experts = tokens // 2
    part = out_ref.shape[0] * CAP
    step = pl.program_id(0)

    @pl.when(step == 0)
    def _():
        copy = pltpu.make_async_copy(coded_hbm, coded_ref, sem)
        copy.start()
        numbers = lax.broadcasted_iota(jnp.int32, (experts, tokens), 0)
        first = routes_ref[0:1, :] == numbers
        second = routes_ref[1:2, :] == numbers
        named = jnp.where(first | second, 1.0, 0.0)
        earlier = lax.broadcasted_iota(jnp.int32, (tokens, tokens), 0) < lax.broadcasted_iota(jnp.int32, (tokens, tokens), 1)
        rank = jnp.dot(
            named.astype(jnp.bfloat16),
            jnp.where(earlier, 1.0, 0.0).astype(jnp.bfloat16),
            preferred_element_type=jnp.float32,
        )
        weight = jnp.where(first, weight_ref[0:1, :], 0.0) + jnp.where(second, weight_ref[1:2, :], 0.0)
        slots = lax.broadcasted_iota(jnp.int32, (experts, CAP, tokens), 1).astype(jnp.float32)
        slot_of = jnp.where(named > 0.0, rank, -1.0)
        pick = jnp.broadcast_to(slot_of[:, None, :], (experts, CAP, tokens)) == slots
        pick_ref[...] = jnp.where(pick, 1.0, 0.0).astype(jnp.bfloat16).reshape(experts * CAP, tokens)
        spread = jnp.broadcast_to(weight[:, None, :], (experts, CAP, tokens))
        slot_weight_ref[...] = jnp.sum(jnp.where(pick, spread, 0.0).reshape(experts * CAP, tokens), axis=1, keepdims=True)
        place = numbers.astype(jnp.float32) * (2 * CAP) + rank
        place_ref[0:1, :] = jnp.sum(jnp.where(first, place, 0.0), axis=0, keepdims=True)
        place_ref[1:2, :] = jnp.sum(jnp.where(second, place, 0.0), axis=0, keepdims=True)
        copy.wait()
        for b in range(blocks):
            columns = pl.ds(b * size, size)
            scale = row_to_column(scale_ref[b : b + 1, :], tokens)
            inputs_ref[:, columns] = (coded_ref[:, columns].astype(jnp.float32) * scale).astype(jnp.bfloat16)

    pick = pick_ref[pl.ds(pl.multiple_of(step * part, part), part), :]
    rows = jnp.dot(pick, inputs_ref[...], preferred_element_type=jnp.float32).astype(jnp.bfloat16)
    rows = rows.reshape(-1, CAP, width)
    out_ref[:, 0] = rows
    out_ref[:, 1] = rows


def prepare(coded, scale, routes, weight, steps=4):
    tokens, width = coded.shape
    experts = tokens // 2
    whole = lambda i: (0, 0)
    return pl.pallas_call(
        prepare_kernel,
        grid=(steps,),
        in_specs=[
            pl.BlockSpec(memory_space=pl.ANY),
            pl.BlockSpec(scale.shape, whole),
            pl.BlockSpec(routes.shape, whole),
            pl.BlockSpec(weight.shape, whole),
        ],
        out_specs=(
            pl.BlockSpec((experts // steps, 2, CAP, width), lambda i: (i, 0, 0, 0)),
            pl.BlockSpec((experts * CAP, tokens), whole),
            pl.BlockSpec((experts * CAP, 1), whole),
            pl.BlockSpec((2, tokens), whole),
        ),
        out_shape=(
            jax.ShapeDtypeStruct((experts, 2, CAP, width), jnp.bfloat16),
            jax.ShapeDtypeStruct((experts * CAP, tokens), jnp.bfloat16),
            jax.ShapeDtypeStruct((experts * CAP, 1), jnp.float32),
            jax.ShapeDtypeStruct((2, tokens), jnp.float32),
        ),
        scratch_shapes=[
            pltpu.VMEM((tokens, width), jnp.bfloat16),
            pltpu.VMEM((tokens, width), jnp.bfloat16),
            pltpu.SemaphoreType.DMA(()),
        ],
        compiler_params=pltpu.CompilerParams(vmem_limit_bytes=VMEM_LIMIT),
        name="prepare",
    )(coded, scale, routes, weight)


def select_kernel(place_ref, first_ref, second_ref, both_ref):
    tokens = place_ref.shape[1]
    rows = first_ref.shape[1]
    numbers = lax.broadcasted_iota(jnp.int32, (tokens, rows), 1)
    numbers = (numbers - jnp.where((numbers & CAP) != 0, CAP, 0)).astype(jnp.float32)
    first = jnp.where(numbers == row_to_column(place_ref[0:1, :], tokens), 1.0, 0.0)
    second = jnp.where(numbers == row_to_column(place_ref[1:2, :], tokens), 1.0, 0.0)
    first_ref[...] = first.astype(jnp.bfloat16)
    second_ref[...] = second.astype(jnp.bfloat16)
    both_ref[...] = (first + second).astype(jnp.bfloat16)


def select(place):
    tokens = place.shape[1]
    shape = jax.ShapeDtypeStruct((tokens, tokens * CAP), jnp.bfloat16)
    return pl.pallas_call(select_kernel, out_shape=(shape,) * 3, name="select")(place)


def send_cot_kernel(cot_ref, pick_ref, weight_ref, out_ref):
    rows = jnp.dot(pick_ref[...], cot_ref[...], preferred_element_type=jnp.float32)
    rows = (rows * weight_ref[...]).astype(jnp.bfloat16).reshape(-1, CAP, cot_ref.shape[1])
    out_ref[:, 0] = rows
    out_ref[:, 1] = rows


def send_cot(cotangent, pick, slot_weight, steps=4):
    tokens, width = cotangent.shape
    experts = pick.shape[0] // CAP
    return pl.pallas_call(
        send_cot_kernel,
        grid=(steps,),
        in_specs=[
            pl.BlockSpec(cotangent.shape, lambda i: (0, 0)),
            pl.BlockSpec((experts * CAP // steps, tokens), lambda i: (i, 0)),
            pl.BlockSpec((experts * CAP // steps, 1), lambda i: (i, 0)),
        ],
        out_specs=pl.BlockSpec((experts // steps, 2, CAP, width), lambda i: (i, 0, 0, 0)),
        out_shape=jax.ShapeDtypeStruct((experts, 2, CAP, width), jnp.bfloat16),
        compiler_params=pltpu.CompilerParams(vmem_limit_bytes=VMEM_LIMIT),
        cost_estimate=pl.CostEstimate(flops=2 * experts * CAP * tokens * width, bytes_accessed=10_000_000, transcendentals=0),
        name="send_cot",
    )(cotangent, pick, slot_weight)


def finish_out_kernel(back_ref, first_ref, second_ref, weight_ref, cot_ref, out_ref, grad_ref):
    tokens, part = out_ref.shape
    rows = back_ref[...].reshape(-1, part)
    first = jnp.dot(first_ref[...], rows, preferred_element_type=jnp.float32)
    second = jnp.dot(second_ref[...], rows, preferred_element_type=jnp.float32)
    first = first.astype(jnp.bfloat16).astype(jnp.float32)
    second = second.astype(jnp.bfloat16).astype(jnp.float32)
    cot = cot_ref[...].astype(jnp.float32)
    total = first * row_to_column(weight_ref[0:1, :], tokens) + second * row_to_column(weight_ref[1:2, :], tokens)
    out_ref[...] = total.astype(jnp.bfloat16)

    @pl.when(pl.program_id(0) == 0)
    def _():
        grad_ref[...] = jnp.zeros_like(grad_ref)

    grad_ref[0:1, :] += column_to_row(jnp.sum(cot * first, axis=1, keepdims=True), tokens)
    grad_ref[1:2, :] += column_to_row(jnp.sum(cot * second, axis=1, keepdims=True), tokens)


def finish_out(back, first, second, weight, cotangent, steps=4):
    nodes, cap, width = back.shape
    tokens = cotangent.shape[0]
    part = width // steps
    whole = lambda i: (0, 0)
    return pl.pallas_call(
        finish_out_kernel,
        grid=(steps,),
        in_specs=[
            pl.BlockSpec((nodes, cap, part), lambda i: (0, 0, i)),
            pl.BlockSpec(first.shape, whole),
            pl.BlockSpec(second.shape, whole),
            pl.BlockSpec(weight.shape, whole),
            pl.BlockSpec((tokens, part), lambda i: (0, i)),
        ],
        out_specs=(
            pl.BlockSpec((tokens, part), lambda i: (0, i)),
            pl.BlockSpec((2, tokens), whole),
        ),
        out_shape=(
            jax.ShapeDtypeStruct((tokens, width), jnp.bfloat16),
            jax.ShapeDtypeStruct((2, tokens), jnp.float32),
        ),
        compiler_params=pltpu.CompilerParams(vmem_limit_bytes=VMEM_LIMIT),
        cost_estimate=pl.CostEstimate(flops=4 * nodes * cap * tokens * width, bytes_accessed=10_000_000, transcendentals=0),
        name="finish_out",
    )(back, first, second, weight, cotangent)


def finish_in_kernel(back_ref, both_ref, out_ref):
    rows = back_ref[...].reshape(-1, out_ref.shape[1])
    out_ref[...] = jnp.dot(both_ref[...], rows, preferred_element_type=jnp.float32).astype(jnp.bfloat16)


def finish_in(back, both, steps=4):
    nodes, cap, width = back.shape
    tokens = both.shape[0]
    part = width // steps
    return pl.pallas_call(
        finish_in_kernel,
        grid=(steps,),
        in_specs=[
            pl.BlockSpec((nodes, cap, part), lambda i: (0, 0, i)),
            pl.BlockSpec(both.shape, lambda i: (0, 0)),
        ],
        out_specs=pl.BlockSpec((tokens, part), lambda i: (0, i)),
        out_shape=jax.ShapeDtypeStruct((tokens, width), jnp.bfloat16),
        compiler_params=pltpu.CompilerParams(vmem_limit_bytes=VMEM_LIMIT),
        name="finish_in",
    )(back, both)


def dot(a, b, a_dim, b_dim):
    return lax.dot_general(a, b, (((a_dim,), (b_dim,)), ((), ())), preferred_element_type=jnp.float32)


def exchange(rows):
    return lax.all_to_all(rows, AXES, split_axis=0, concat_axis=0, tiled=True)


def on_device(coded, block_scale, routes, route_weight, cotangent, w_gate, w_up, w_down):
    tokens, width = coded.shape
    nodes = lax.axis_size(AXES)
    weight = route_weight.T
    gate_w, up_w, down_w = w_gate[0].T, w_up[0].T, w_down[0]

    send_rows, pick, slot_weight, place = prepare(coded, block_scale.T, routes.T, weight)
    rows = exchange(send_rows.reshape(nodes, CAP, width))
    cot_rows = exchange(send_cot(cotangent, pick, slot_weight).reshape(nodes, CAP, width))
    rows = rows.reshape(-1, width)
    cot_rows = cot_rows.reshape(-1, width)

    gate = dot(rows, gate_w, 1, 1)
    upper = dot(rows, up_w, 1, 1)
    sigma = jax.nn.sigmoid(gate)
    active = gate * sigma
    hidden = (active * upper).astype(jnp.bfloat16)
    partial_out = dot(hidden, down_w, 1, 0).astype(jnp.bfloat16)
    partial_out, cot_rows = lax.optimization_barrier((partial_out, cot_rows))
    back_out = exchange(partial_out.reshape(nodes, CAP, width))

    d_hidden = dot(cot_rows, down_w, 1, 1)
    d_upper = (d_hidden * active).astype(jnp.bfloat16)
    d_gate = (d_hidden * upper * sigma * (1.0 + gate * (1.0 - sigma))).astype(jnp.bfloat16)
    partial_in = (dot(d_gate, gate_w, 1, 0) + dot(d_upper, up_w, 1, 0)).astype(jnp.bfloat16)
    back_in = exchange(partial_in.reshape(nodes, CAP, width))

    grad_down = dot(hidden, cot_rows, 0, 0).astype(jnp.bfloat16)
    grad_gate = dot(d_gate, rows, 0, 0).astype(jnp.bfloat16)
    grad_up = dot(d_upper, rows, 0, 0).astype(jnp.bfloat16)

    first, second, both = select(place)
    layer_out, grad_weight = finish_out(back_out, first, second, weight, cotangent)
    grad_input = finish_in(back_in, both)
    return (layer_out, grad_input, grad_weight.T, grad_gate.T[None], grad_up.T[None], grad_down[None])


def solution(mesh):
    rows = P(AXES, None)
    matrix = P(AXES, None, None)
    return jax.shard_map(
        on_device,
        mesh=mesh,
        in_specs=(rows, rows, rows, rows, rows, matrix, matrix, matrix),
        out_specs=(rows, rows, rows, matrix, matrix, matrix),
        check_vma=False,
    )
```

time: 264 us -> 262 us (level)
  blocking collectives: 0 us -> 56.9 us
  waiting for transfers between devices: 153 us -> 104 us
  local copies, waits for them, and re-layouts: 8.75 us -> 1.22 us
  Pallas kernels: 14.3 us -> 21.6 us
  starting transfers between devices: 26.8 us -> 21.6 us
  matrix products: 59.1 us -> 54.4 us
    all_to_all x0 -> x1, blocking collectives: none -> 56.9 us  [exchange(): return lax.all_to_all(rows, AXES, split_axis=0, concat_axis=0, tiled=True)]
    all_to_all x4 -> x3, waiting for transfers between devices: 153 us -> 104 us  [exchange(): return lax.all_to_all(rows, AXES, split_axis=0, concat_axis=0, tiled=True)]
    unnamed x40 -> x24, local copies, waits for them, and re-layouts: 8.75 us -> 1.22 us
    all_to_all x4 -> x3, starting transfers between devices: 26.8 us -> 21.6 us  [exchange(): return lax.all_to_all(rows, AXES, split_axis=0, concat_axis=0, tiled=True)]
    dot_general x9, matrix products: 59.1 us -> 54.4 us  [dot(): lax.dot_general(a, b, (((a_dim,), (b_dim,)), ((), ())), preferred_element...]
    pallas_call x3, Pallas kernels: 8.08 us -> 11.8 us  [the longest x1 5.4 us: prepare(): pl.pallas_call(prepare_kernel, grid=(steps,), in_specs=[pl.BlockSpec(memo...]
    pallas_call x1, Pallas kernels: 1.19 us -> 4.55 us  [send_cot(): pl.pallas_call(send_cot_kernel, grid=(steps,), in_specs=[pl.BlockSpec(cot...]
  transfers between devices with their start and end apart: 4 -> 3, of which waited for: 4 -> 3; matrix products, arithmetic and copies ran while one was open for 17% -> 15% of each run, Pallas kernels for 2% -> 4%
where the time goes in v1:
time: 262 us; the launch traced here: 261 us
  waiting for transfers between devices  104 us (40%)
  blocking collectives  56.9 us (22%)
  matrix products  54.4 us (21%)
  Pallas kernels  21.6 us (8%)
  starting transfers between devices  21.6 us (8%)
    all_to_all x3, waiting for transfers between devices, exchange(): return lax.all_to_all(rows, AXES, split_axis=0, concat_axis=0, tiled=True)  104 us
    all_to_all x1, blocking collectives, exchange(): return lax.all_to_all(rows, AXES, split_axis=0, concat_axis=0, tiled=True)  56.9 us
    dot_general x9, matrix products, dot(): lax.dot_general(a, b, (((a_dim,), (b_dim,)), ((), ())), preferred_element...  54.4 us
    all_to_all x3, starting transfers between devices, exchange(): return lax.all_to_all(rows, AXES, split_axis=0, concat_axis=0, tiled=True)  21.6 us
    pallas_call x1, Pallas kernels, prepare(): pl.pallas_call(prepare_kernel, grid=(steps,), in_specs=[pl.BlockSpec(memo...  5.4 us
  transfers between devices with their start and end apart: 3, of which 3 were waited for; matrix products, arithmetic and copies ran while one was open for 15% of the time, Pallas kernels for 4%

profile of v1, /device:TPU:7, one launch (start us, length us, event | category | flops | bytes accessed | tf_op | source)
XLA Modules:
  0.0 261.1 jit_solution(8662601046258380198)
XLA Ops:
  0.6 0.0 copy-start
  0.6 5.4 %prepare.1 = (bf16[64,2,8,2048]{3,2,1,0:T(8,128)(2,1)}, bf16[512,128]{1,0:T(8,128)(2,1)}, f32[512,1]{1,0:T(8,128)}, f32[2,128]{1,0:T(2,128)}) custom-call(bf16[128,2048]{1,0:T(8,128)(2,1)} %coded_hbm.1, f32[16,128]{1,0:T(8,128)} %bitcast.65, s32[2,128]{1,0:T(2,128)} %bitcast.68, f32[2,128]{1,0:T(2,128)} %bitcast.66), custom_call_target="tpu_custom_call" | custom-call | tf_op jit(solution)/shard_map/prepare/pallas_call | solution.py:72
  6.1 11.2 %all-to-all-start = ((bf16[128,8,2048]{2,1,0:T(8,128)(2,1)}), bf16[128,8,2048]{2,1,0:T(8,128)(2,1)}, u32[]{:S(2)}, u32[]{:S(2)}) async-start(bf16[128,8,2048]{2,1,0:T(8,128)(2,1)} %bitcast.64), calls=%async_computation | async-start | bytes 8388608 | tf_op jit(solution)/shard_map/all_to_all | solution.py:223
  17.3 4.6 %send_cot.1 = bf16[64,2,8,2048]{3,2,1,0:T(8,128)(2,1)} custom-call(bf16[128,2048]{1,0:T(8,128)(2,1)} %cot_ref.3, bf16[512,128]{1,0:T(8,128)(2,1)} %get-tuple-element.18.pick_ref, f32[512,1]{1,0:T(8,128)} %get-tuple-element.19.weight_ref), custom_call_target="tpu_custom_call" | custom-call | flops 268435456 | bytes 10000000 | tf_op jit(solution)/shard_map/send_cot/pallas_call | solution.py:131
  21.9 47.4 %all-to-all-done = bf16[128,8,2048]{2,1,0:T(8,128)(2,1)} async-done(((bf16[128,8,2048]{2,1,0:T(8,128)(2,1)}), bf16[128,8,2048]{2,1,0:T(8,128)(2,1)}, u32[]{:S(2)}, u32[]{:S(2)}) %all-to-all-start) | async-done | bytes 4194336 | tf_op jit(solution)/shard_map/all_to_all | solution.py:223
  69.2 5.2 %all-to-all-start.1 = ((bf16[128,8,2048]{2,1,0:T(8,128)(2,1)}), bf16[128,8,2048]{2,1,0:T(8,128)(2,1)}, u32[]{:S(2)}, u32[]{:S(2)}) async-start(bf16[128,8,2048]{2,1,0:T(8,128)(2,1)} %bitcast.62), calls=%async_computation.1 | async-start | bytes 8388608 | tf_op jit(solution)/shard_map/all_to_all | solution.py:223
  74.4 0.0 copy-start.3
  74.4 6.0 %fusion.7 = f32[1024,704]{0,1:T(8,128)S(1)} fusion(bf16[128,8,2048]{2,1,0:T(8,128)(2,1)} %all-to-all-done, bf16[1,2048,704]{1,2,0:T(8,128)(2,1)} %param.13), kind=kOutput, calls=%fused_computation.8 | convolution fusion | flops 2952790016 | bytes 9961472 | tf_op jit(solution)/shard_map/dot_general | solution.py:219
  80.5 0.0 copy-done.3
  80.5 0.0 copy-start.7
  80.5 8.1 %multiply_convert_fusion.2 = (bf16[1024,704]{0,1:T(8,128)(2,1)S(1)}, f32[1024,704]{0,1:T(8,128)}) fusion(f32[1024,704]{0,1:T(8,128)S(1)} %fusion.7, bf16[1,2048,704]{1,2,0:T(8,128)(2,1)S(1)} %copy-done.3, bf16[128,8,2048]{2,1,0:T(8,128)(2,1)} %all-to-all-done), kind=kOutput, calls=%fused_computation.27 | convolution fusion | flops 2957115392 | bytes 14286848 | tf_op jit(solution)/shard_map/dot_general | solution.py:219
  88.6 0.0 copy-done.7
  88.6 0.0 copy-start.10
  88.6 1.2 copy-done.10
  89.8 0.0 copy-done
  89.8 5.1 %convolution_convert_fusion = bf16[1024,2048]{1,0:T(8,128)(2,1)} fusion(bf16[1024,704]{0,1:T(8,128)(2,1)S(1)} %get-tuple-element.30, bf16[1,704,2048]{2,1,0:T(8,128)(2,1)S(1)} %copy-done), kind=kOutput, calls=%fused_computation.10 | convolution fusion | flops 2954887168 | bytes 8519680 | tf_op jit(solution)/shard_map/dot_general | solution.py:219
  94.8 31.5 %all-to-all-done.1 = bf16[128,8,2048]{2,1,0:T(8,128)(2,1)} async-done(((bf16[128,8,2048]{2,1,0:T(8,128)(2,1)}), bf16[128,8,2048]{2,1,0:T(8,128)(2,1)}, u32[]{:S(2)}, u32[]{:S(2)}) %all-to-all-start.1) | async-done | bytes 4194336 | tf_op jit(solution)/shard_map/all_to_all | solution.py:223
  126.4 0.0 copy-start.2
  126.4 7.4 %multiply_convert_fusion = (bf16[1024,704]{0,1:T(8,128)(2,1)S(1)}, bf16[1024,704]{0,1:T(8,128)(2,1)S(1)}) fusion(f32[1024,704]{0,1:T(8,128)} %copy-done.7, f32[1024,704]{0,1:T(8,128)} %get-tuple-element.31, bf16[1024,2048]{1,0:T(8,128)(2,1)} %bitcast.9, bf16[1,704,2048]{2,1,0:T(8,128)(2,1)S(1)} %copy-done), kind=kOutput, calls=%fused_computation.25 | convolution fusion | flops 2962161664 | bytes 15728640 | tf_op jit(solution)/shard_map/dot_general | solution.py:219
  133.7 0.0 copy-start.5
  133.8 0.0 copy-start.8
  133.8 0.0 copy-done.2
  133.8 0.0 copy-start.4
  133.8 3.5 %fusion.27 = f32[1024,2048]{1,0:T(8,128)S(1)} fusion(bf16[1024,704]{0,1:T(8,128)(2,1)S(1)} %get-tuple-element.29, bf16[1,2048,704]{1,2,0:T(8,128)(2,1)S(1)} %copy-done.2), kind=kOutput, calls=%fused_computation.22 | convolution fusion | flops 2952790016 | bytes 12713984 | tf_op jit(solution)/shard_map/dot_general | solution.py:219
  137.3 0.0 copy-done.5
  137.3 0.0 copy-done.8
  137.4 0.0 copy-done.4
  137.4 4.3 %fusion = bf16[128,8,2048]{2,1,0:T(8,128)(2,1)S(1)} fusion(f32[1024,2048]{1,0:T(8,128)S(1)} %fusion.27, bf16[1024,704]{0,1:T(8,128)(2,1)S(1)} %get-tuple-element.28, bf16[1,2048,704]{1,2,0:T(8,128)(2,1)S(1)} %copy-done.4), kind=kOutput, calls=%fused_computation.1 | convolution fusion | flops 2956984320 | bytes 16908288 | tf_op jit(solution)/shard_map/dot_general | solution.py:219
  141.6 56.9 %all_to_all.20.back_ref = bf16[128,8,2048]{2,1,0:T(8,128)(2,1)} all-to-all(bf16[128,8,2048]{2,1,0:T(8,128)(2,1)S(1)} %fusion), channel_id=1, replica_groups=mesh['dp'=8,'expert'=16] {'dp','expert'}, dimensions={0} | all-to-all | bytes 8388608 | tf_op jit(solution)/shard_map/all_to_all | solution.py:223
  198.6 0.0 copy-start.11
  198.6 5.2 %all-to-all-start.2 = ((bf16[128,8,2048]{2,1,0:T(8,128)(2,1)}), bf16[128,8,2048]{2,1,0:T(8,128)(2,1)}, u32[]{:S(2)}, u32[]{:S(2)}) async-start(bf16[128,8,2048]{2,1,0:T(8,128)(2,1)} %bitcast.63), calls=%async_computation.2 | async-start | bytes 8388608 | tf_op jit(solution)/shard_map/all_to_all | solution.py:223
  203.7 1.7 select.1
  205.5 0.0 copy-done.11
  205.5 0.0 copy-start.9
  205.5 6.7 %fusion.15 = bf16[1,704,2048]{2,1,0:T(8,128)(2,1)} fusion(bf16[1024,704]{0,1:T(8,128)(2,1)S(1)} %copy-done.11, bf16[1024,2048]{1,0:T(8,128)(2,1)} %bitcast.9), kind=kOutput, calls=%fused_computation.14 | convolution fusion | flops 2954231808 | bytes 8519680 | tf_op jit(solution)/shard_map/dot_general | solution.py:219
  212.2 0.0 copy-done.9
  212.2 0.0 copy-start.6
  212.2 6.7 %fusion.19 = bf16[1,2048,704]{1,2,0:T(8,128)(2,1)} fusion(bf16[1024,704]{0,1:T(8,128)(2,1)S(1)} %copy-done.9, bf16[128,8,2048]{2,1,0:T(8,128)(2,1)} %all-to-all-done), kind=kOutput, calls=%fused_computation.16 | convolution fusion | flops 2954231808 | bytes 8519680 | tf_op jit(solution)/shard_map/dot_general | solution.py:219
  218.9 0.0 copy-done.6
  219.0 6.6 %fusion.16 = bf16[1,2048,704]{1,2,0:T(8,128)(2,1)} fusion(bf16[1024,704]{0,1:T(8,128)(2,1)S(1)} %copy-done.6, bf16[128,8,2048]{2,1,0:T(8,128)(2,1)} %all-to-all-done), kind=kOutput, calls=%fused_computation.15 | convolution fusion | flops 2954231808 | bytes 8519680 | tf_op jit(solution)/shard_map/dot_general | solution.py:219
  225.6 0.0 copy-start.1
  225.6 4.7 %finish_in.1 = bf16[128,2048]{1,0:T(8,128)(2,1)} custom-call(bf16[128,8,2048]{2,1,0:T(8,128)(2,1)} %all_to_all.20.back_ref, bf16[128,1024]{1,0:T(8,128)(2,1)} %get-tuple-element.26.both_ref), custom_call_target="tpu_custom_call" | custom-call | tf_op jit(solution)/shard_map/finish_in/pallas_call | solution.py:204
  230.2 25.4 %all-to-all-done.2.back_ref = bf16[128,8,2048]{2,1,0:T(8,128)(2,1)} async-done(((bf16[128,8,2048]{2,1,0:T(8,128)(2,1)}), bf16[128,8,2048]{2,1,0:T(8,128)(2,1)}, u32[]{:S(2)}, u32[]{:S(2)}) %all-to-all-start.2) | async-done | bytes 4194336 | tf_op jit(solution)/shard_map/all_to_all | solution.py:223
  255.7 5.2 %finish_out.1 = (bf16[128,2048]{1,0:T(8,128)(2,1)}, f32[2,128]{1,0:T(2,128)}) custom-call(bf16[128,8,2048]{2,1,0:T(8,128)(2,1)} %all-to-all-done.2.back_ref, bf16[128,1024]{1,0:T(8,128)(2,1)} %get-tuple-element.22.first_ref, bf16[128,1024]{1,0:T(8,128)(2,1)} %get-tuple-element.23.second_ref, f32[2,128]{1,0:T(2,128)} %bitcast.67, bf16[128,2048]{1,0:T(8,128)(2,1)} %cot_ref.3), custom_call_target="tpu_custom_call" | custom-call | flops 1073741824 | bytes 10000000 | tf_op jit(solution)/shard_map/finish_out/pallas_call | solution.py:171
  260.9 0.0 copy-done.1
Async XLA Ops:
  0.6 89.1 %copy-start = (bf16[1,704,2048]{2,1,0:T(8,128)(2,1)S(1)}, bf16[1,704,2048]{2,1,0:T(8,128)(2,1)}, u32[]{:S(2)}) copy-start(bf16[1,704,2048]{2,1,0:T(8,128)(2,1)} %param.15) | copy-start | bytes 8650756
  6.1 63.2 %all-to-all-start = ((bf16[128,8,2048]{2,1,0:T(8,128)(2,1)}), bf16[128,8,2048]{2,1,0:T(8,128)(2,1)}, u32[]{:S(2)}, u32[]{:S(2)}) async-start(bf16[128,8,2048]{2,1,0:T(8,128)(2,1)} %bitcast.64), calls=%async_computation | async-start | bytes 8388608 | tf_op jit(solution)/shard_map/all_to_all | solution.py:223
  69.2 57.1 %all-to-all-start.1 = ((bf16[128,8,2048]{2,1,0:T(8,128)(2,1)}), bf16[128,8,2048]{2,1,0:T(8,128)(2,1)}, u32[]{:S(2)}, u32[]{:S(2)}) async-start(bf16[128,8,2048]{2,1,0:T(8,128)(2,1)} %bitcast.62), calls=%async_computation.1 | async-start | bytes 8388608 | tf_op jit(solution)/shard_map/all_to_all | solution.py:223
  74.4 6.0 %copy-start.3 = (bf16[1,2048,704]{1,2,0:T(8,128)(2,1)S(1)}, bf16[1,2048,704]{1,2,0:T(8,128)(2,1)}, u32[]{:S(2)}) copy-start(bf16[1,2048,704]{1,2,0:T(8,128)(2,1)} %param.14) | copy-start | bytes 8650756
  80.5 8.1 %copy-start.7 = (f32[1024,704]{0,1:T(8,128)}, f32[1024,704]{0,1:T(8,128)S(1)}, u32[]{:S(2)}) copy-start(f32[1024,704]{0,1:T(8,128)S(1)} %fusion.7) | copy-start | bytes 8650756
  88.6 1.2 copy-start.10
  126.4 7.4 %copy-start.2 = (bf16[1,2048,704]{1,2,0:T(8,128)(2,1)S(1)}, bf16[1,2048,704]{1,2,0:T(8,128)(2,1)}, u32[]{:S(2)}) copy-start(bf16[1,2048,704]{1,2,0:T(8,128)(2,1)} %param.13) | copy-start | bytes 8650756
  133.7 3.6 %copy-start.5 = (bf16[1024,704]{0,1:T(8,128)(2,1)}, bf16[1024,704]{0,1:T(8,128)(2,1)S(1)}, u32[]{:S(2)}) copy-start(bf16[1024,704]{0,1:T(8,128)(2,1)S(1)} %get-tuple-element.29) | copy-start | bytes 4325380
  133.8 3.6 %copy-start.8 = (bf16[1024,704]{0,1:T(8,128)(2,1)}, bf16[1024,704]{0,1:T(8,128)(2,1)S(1)}, u32[]{:S(2)}) copy-start(bf16[1024,704]{0,1:T(8,128)(2,1)S(1)} %get-tuple-element.28) | copy-start | bytes 4325380
  133.8 3.6 %copy-start.4 = (bf16[1,2048,704]{1,2,0:T(8,128)(2,1)S(1)}, bf16[1,2048,704]{1,2,0:T(8,128)(2,1)}, u32[]{:S(2)}) copy-start(bf16[1,2048,704]{1,2,0:T(8,128)(2,1)} %param.14) | copy-start | bytes 8650756
  198.6 6.9 %copy-start.11 = (bf16[1024,704]{0,1:T(8,128)(2,1)S(1)}, bf16[1024,704]{0,1:T(8,128)(2,1)}, u32[]{:S(2)}) copy-start(bf16[1024,704]{0,1:T(8,128)(2,1)} %copy-done.10) | copy-start | bytes 4325380
  198.6 57.1 %all-to-all-start.2 = ((bf16[128,8,2048]{2,1,0:T(8,128)(2,1)}), bf16[128,8,2048]{2,1,0:T(8,128)(2,1)}, u32[]{:S(2)}, u32[]{:S(2)}) async-start(bf16[128,8,2048]{2,1,0:T(8,128)(2,1)} %bitcast.63), calls=%async_computation.2 | async-start | bytes 8388608 | tf_op jit(solution)/shard_map/all_to_all | solution.py:223
  205.5 6.7 %copy-start.9 = (bf16[1024,704]{0,1:T(8,128)(2,1)S(1)}, bf16[1024,704]{0,1:T(8,128)(2,1)}, u32[]{:S(2)}) copy-start(bf16[1024,704]{0,1:T(8,128)(2,1)} %copy-done.8) | copy-start | bytes 4325380
  212.2 6.7 %copy-start.6 = (bf16[1024,704]{0,1:T(8,128)(2,1)S(1)}, bf16[1024,704]{0,1:T(8,128)(2,1)}, u32[]{:S(2)}) copy-start(bf16[1024,704]{0,1:T(8,128)(2,1)} %copy-done.5) | copy-start | bytes 4325380
  225.6 35.3 %copy-start.1 = (bf16[1,704,2048]{2,1,0:T(8,128)(2,1)S(1)}, bf16[1,704,2048]{2,1,0:T(8,128)(2,1)}, u32[]{:S(2)}) copy-start(bf16[1,704,2048]{2,1,0:T(8,128)(2,1)} %param.15) | copy-start | bytes 8650756

commit v2 on v1

--- a/solution.py
+++ b/solution.py
@@ -65,7 +65,7 @@
     out_ref[:, 1] = rows
 
 
-def prepare(coded, scale, routes, weight, steps=4):
+def prepare(coded, scale, routes, weight, steps=2):
     tokens, width = coded.shape
     experts = tokens // 2
     whole = lambda i: (0, 0)
@@ -197,7 +197,7 @@
     out_ref[...] = jnp.dot(both_ref[...], rows, preferred_element_type=jnp.float32).astype(jnp.bfloat16)
 
 
-def finish_in(back, both, steps=4):
+def finish_in(back, both, steps=2):
     nodes, cap, width = back.shape
     tokens = both.shape[0]
     part = width // steps
@@ -248,6 +248,7 @@
     d_upper = (d_hidden * active).astype(jnp.bfloat16)
     d_gate = (d_hidden * upper * sigma * (1.0 + gate * (1.0 - sigma))).astype(jnp.bfloat16)
     partial_in = (dot(d_gate, gate_w, 1, 0) + dot(d_upper, up_w, 1, 0)).astype(jnp.bfloat16)
+    partial_in, back_out = lax.optimization_barrier((partial_in, back_out))
     back_in = exchange(partial_in.reshape(nodes, CAP, width))
 
     grad_down = dot(hidden, cot_rows, 0, 0).astype(jnp.bfloat16)

time: 262 us -> 244 us (0.931)
  blocking collectives: 56.9 us -> 0 us
  waiting for transfers between devices: 104 us -> 139 us
  starting transfers between devices: 21.6 us -> 26.8 us
    all_to_all x1 -> x0, blocking collectives: 56.9 us -> none  [exchange(): return lax.all_to_all(rows, AXES, split_axis=0, concat_axis=0, tiled=True)]
    all_to_all x3 -> x4, waiting for transfers between devices: 104 us -> 139 us  [exchange(): return lax.all_to_all(rows, AXES, split_axis=0, concat_axis=0, tiled=True)]
    all_to_all x3 -> x4, starting transfers between devices: 21.6 us -> 26.8 us  [exchange(): return lax.all_to_all(rows, AXES, split_axis=0, concat_axis=0, tiled=True)]
  transfers between devices with their start and end apart: 3 -> 4, of which waited for: 3 -> 4; matrix products, arithmetic and copies ran while one was open for 15% -> 23% of each run, Pallas kernels for 4% -> 5%
where the time goes in v2:
time: 244 us
  waiting for transfers between devices  139 us (57%)
  matrix products  55.6 us (23%)
  starting transfers between devices  26.8 us (11%)
  Pallas kernels  20.1 us (8%)
    all_to_all x4, waiting for transfers between devices, exchange(): return lax.all_to_all(rows, AXES, split_axis=0, concat_axis=0, tiled=True)  139 us
    dot_general x9, matrix products, dot(): lax.dot_general(a, b, (((a_dim,), (b_dim,)), ((), ())), preferred_element...  55.6 us
    all_to_all x4, starting transfers between devices, exchange(): return lax.all_to_all(rows, AXES, split_axis=0, concat_axis=0, tiled=True)  26.8 us
    pallas_call x1, Pallas kernels, finish_out(): pl.pallas_call(finish_out_kernel, grid=(steps,), in_specs=[pl.BlockSpec((...  5.35 us
    pallas_call x1, Pallas kernels, prepare(): pl.pallas_call(prepare_kernel, grid=(steps,), in_specs=[pl.BlockSpec(memo...  4.92 us
  transfers between devices with their start and end apart: 4, of which 4 were waited for; matrix products, arithmetic and copies ran while one was open for 23% of the time, Pallas kernels for 5%

profile of v2, /device:TPU:7, one launch (start us, length us, event | category | flops | bytes accessed | tf_op | source)
XLA Modules:
  0.0 243.6 jit_solution(1478064988993952668)
XLA Ops:
  0.6 0.0 copy-start
  0.6 4.9 %prepare.1 = (bf16[64,2,8,2048]{3,2,1,0:T(8,128)(2,1)}, bf16[512,128]{1,0:T(8,128)(2,1)}, f32[512,1]{1,0:T(8,128)}, f32[2,128]{1,0:T(2,128)}) custom-call(bf16[128,2048]{1,0:T(8,128)(2,1)} %coded_hbm.1, f32[16,128]{1,0:T(8,128)} %bitcast.65, s32[2,128]{1,0:T(2,128)} %bitcast.68, f32[2,128]{1,0:T(2,128)} %bitcast.66), custom_call_target="tpu_custom_call" | custom-call | tf_op jit(solution)/shard_map/prepare/pallas_call | solution.py:72
  5.6 11.3 %all-to-all-start = ((bf16[128,8,2048]{2,1,0:T(8,128)(2,1)}), bf16[128,8,2048]{2,1,0:T(8,128)(2,1)}, u32[]{:S(2)}, u32[]{:S(2)}) async-start(bf16[128,8,2048]{2,1,0:T(8,128)(2,1)} %bitcast.64), calls=%async_computation | async-start | bytes 8388608 | tf_op jit(solution)/shard_map/all_to_all | solution.py:223
  16.8 4.6 %send_cot.1 = bf16[64,2,8,2048]{3,2,1,0:T(8,128)(2,1)} custom-call(bf16[128,2048]{1,0:T(8,128)(2,1)} %cot_ref.3, bf16[512,128]{1,0:T(8,128)(2,1)} %get-tuple-element.20.pick_ref, f32[512,1]{1,0:T(8,128)} %get-tuple-element.21.weight_ref), custom_call_target="tpu_custom_call" | custom-call | flops 268435456 | bytes 10000000 | tf_op jit(solution)/shard_map/send_cot/pallas_call | solution.py:131
  21.4 47.3 %all-to-all-done = bf16[128,8,2048]{2,1,0:T(8,128)(2,1)} async-done(((bf16[128,8,2048]{2,1,0:T(8,128)(2,1)}), bf16[128,8,2048]{2,1,0:T(8,128)(2,1)}, u32[]{:S(2)}, u32[]{:S(2)}) %all-to-all-start) | async-done | bytes 4194336 | tf_op jit(solution)/shard_map/all_to_all | solution.py:223
  68.8 5.2 %all-to-all-start.1 = ((bf16[128,8,2048]{2,1,0:T(8,128)(2,1)}), bf16[128,8,2048]{2,1,0:T(8,128)(2,1)}, u32[]{:S(2)}, u32[]{:S(2)}) async-start(bf16[128,8,2048]{2,1,0:T(8,128)(2,1)} %bitcast.61), calls=%async_computation.1 | async-start | bytes 8388608 | tf_op jit(solution)/shard_map/all_to_all | solution.py:223
  73.9 0.0 copy-start.3
  74.0 6.0 %fusion.6 = f32[1024,704]{0,1:T(8,128)S(1)} fusion(bf16[128,8,2048]{2,1,0:T(8,128)(2,1)} %all-to-all-done, bf16[1,2048,704]{1,2,0:T(8,128)(2,1)} %param.13), kind=kOutput, calls=%fused_computation.7 | convolution fusion | flops 2952790016 | bytes 9961472 | tf_op jit(solution)/shard_map/dot_general | solution.py:219
  80.0 0.0 copy-done.3
  80.0 0.0 copy-start.7
  80.0 8.1 %multiply_convert_fusion.2 = (bf16[1024,704]{0,1:T(8,128)(2,1)S(1)}, f32[1024,704]{0,1:T(8,128)}) fusion(f32[1024,704]{0,1:T(8,128)S(1)} %fusion.6, bf16[1,2048,704]{1,2,0:T(8,128)(2,1)S(1)} %copy-done.3, bf16[128,8,2048]{2,1,0:T(8,128)(2,1)} %all-to-all-done), kind=kOutput, calls=%fused_computation.26 | convolution fusion | flops 2957115392 | bytes 14286848 | tf_op jit(solution)/shard_map/dot_general | solution.py:219
  88.1 0.0 copy-done.7
  88.1 0.0 copy-start.10
  88.1 1.1 copy-done.10
  89.3 0.0 copy-done
  89.3 5.0 %convolution_convert_fusion = bf16[1024,2048]{1,0:T(8,128)(2,1)} fusion(bf16[1024,704]{0,1:T(8,128)(2,1)S(1)} %get-tuple-element.34, bf16[1,704,2048]{2,1,0:T(8,128)(2,1)S(1)} %copy-done), kind=kOutput, calls=%fused_computation.9 | convolution fusion | flops 2954887168 | bytes 8519680 | tf_op jit(solution)/shard_map/dot_general | solution.py:219
  94.3 31.6 %all-to-all-done.1 = bf16[128,8,2048]{2,1,0:T(8,128)(2,1)} async-done(((bf16[128,8,2048]{2,1,0:T(8,128)(2,1)}), bf16[128,8,2048]{2,1,0:T(8,128)(2,1)}, u32[]{:S(2)}, u32[]{:S(2)}) %all-to-all-start.1) | async-done | bytes 4194336 | tf_op jit(solution)/shard_map/all_to_all | solution.py:223
  125.9 5.2 %all-to-all-start.2 = ((bf16[128,8,2048]{2,1,0:T(8,128)(2,1)}), bf16[128,8,2048]{2,1,0:T(8,128)(2,1)}, u32[]{:S(2)}, u32[]{:S(2)}) async-start(bf16[128,8,2048]{2,1,0:T(8,128)(2,1)} %bitcast.63), calls=%async_computation.2 | async-start | bytes 8388608 | tf_op jit(solution)/shard_map/all_to_all | solution.py:223
  131.1 0.0 copy-start.2
  131.1 7.4 %multiply_convert_fusion = (bf16[1024,704]{0,1:T(8,128)(2,1)S(1)}, bf16[1024,704]{0,1:T(8,128)(2,1)S(1)}) fusion(f32[1024,704]{0,1:T(8,128)} %copy-done.7, f32[1024,704]{0,1:T(8,128)} %get-tuple-element.35, bf16[1024,2048]{1,0:T(8,128)(2,1)} %bitcast.9, bf16[1,704,2048]{2,1,0:T(8,128)(2,1)S(1)} %copy-done), kind=kOutput, calls=%fused_computation.24 | convolution fusion | flops 2962161664 | bytes 15728640 | tf_op jit(solution)/shard_map/dot_general | solution.py:219
  138.5 0.0 copy-start.5
  138.5 0.0 copy-start.8
  138.5 0.0 copy-done.2
  138.5 0.0 copy-start.4
  138.5 3.5 %fusion.26 = f32[1024,2048]{1,0:T(8,128)S(1)} fusion(bf16[1024,704]{0,1:T(8,128)(2,1)S(1)} %get-tuple-element.33, bf16[1,2048,704]{1,2,0:T(8,128)(2,1)S(1)} %copy-done.2), kind=kOutput, calls=%fused_computation.21 | convolution fusion | flops 2952790016 | bytes 12713984 | tf_op jit(solution)/shard_map/dot_general | solution.py:219
  142.1 0.0 copy-done.5
  142.1 0.0 copy-done.8
  142.1 0.0 copy-done.4
  142.1 5.4 %add_convert_fusion = bf16[1024,2048]{1,0:T(8,128)(2,1)} fusion(f32[1024,2048]{1,0:T(8,128)S(1)} %fusion.26, bf16[1024,704]{0,1:T(8,128)(2,1)S(1)} %get-tuple-element.32, bf16[1,2048,704]{1,2,0:T(8,128)(2,1)S(1)} %copy-done.4), kind=kOutput, calls=%fused_computation | convolution fusion | flops 2956984320 | bytes 16908288 | tf_op jit(solution)/shard_map/dot_general | solution.py:219
  147.5 35.5 %all-to-all-done.2.back_ref = bf16[128,8,2048]{2,1,0:T(8,128)(2,1)} async-done(((bf16[128,8,2048]{2,1,0:T(8,128)(2,1)}), bf16[128,8,2048]{2,1,0:T(8,128)(2,1)}, u32[]{:S(2)}, u32[]{:S(2)}) %all-to-all-start.2) | async-done | bytes 4194336 | tf_op jit(solution)/shard_map/all_to_all | solution.py:223
  183.0 0.0 copy-start.11
  183.0 5.2 %all-to-all-start.3 = ((bf16[128,8,2048]{2,1,0:T(8,128)(2,1)}), bf16[128,8,2048]{2,1,0:T(8,128)(2,1)}, u32[]{:S(2)}, u32[]{:S(2)}) async-start(bf16[128,8,2048]{2,1,0:T(8,128)(2,1)} %bitcast.62), calls=%async_computation.3 | async-start | bytes 8388608 | tf_op jit(solution)/shard_map/all_to_all | solution.py:223
  188.2 1.8 select.1
  189.9 0.0 copy-done.11
  189.9 0.0 copy-start.9
  189.9 6.7 %fusion.14 = bf16[1,704,2048]{2,1,0:T(8,128)(2,1)} fusion(bf16[1024,704]{0,1:T(8,128)(2,1)S(1)} %copy-done.11, bf16[1024,2048]{1,0:T(8,128)(2,1)} %bitcast.9), kind=kOutput, calls=%fused_computation.13 | convolution fusion | flops 2954231808 | bytes 8519680 | tf_op jit(solution)/shard_map/dot_general | solution.py:219
  196.7 0.0 copy-done.9
  196.7 0.0 copy-start.6
  196.7 6.7 %fusion.18 = bf16[1,2048,704]{1,2,0:T(8,128)(2,1)} fusion(bf16[1024,704]{0,1:T(8,128)(2,1)S(1)} %copy-done.9, bf16[128,8,2048]{2,1,0:T(8,128)(2,1)} %all-to-all-done), kind=kOutput, calls=%fused_computation.15 | convolution fusion | flops 2954231808 | bytes 8519680 | tf_op jit(solution)/shard_map/dot_general | solution.py:219
  203.4 0.0 copy-done.6
  203.4 6.6 %fusion.15 = bf16[1,2048,704]{1,2,0:T(8,128)(2,1)} fusion(bf16[1024,704]{0,1:T(8,128)(2,1)S(1)} %copy-done.6, bf16[128,8,2048]{2,1,0:T(8,128)(2,1)} %all-to-all-done), kind=kOutput, calls=%fused_computation.14 | convolution fusion | flops 2954231808 | bytes 8519680 | tf_op jit(solution)/shard_map/dot_general | solution.py:219
  210.0 0.0 copy-start.1
  210.0 5.3 %finish_out.1 = (bf16[128,2048]{1,0:T(8,128)(2,1)}, f32[2,128]{1,0:T(2,128)}) custom-call(bf16[128,8,2048]{2,1,0:T(8,128)(2,1)} %all-to-all-done.2.back_ref, bf16[128,1024]{1,0:T(8,128)(2,1)} %get-tuple-element.26.first_ref, bf16[128,1024]{1,0:T(8,128)(2,1)} %get-tuple-element.27.second_ref, f32[2,128]{1,0:T(2,128)} %bitcast.67, bf16[128,2048]{1,0:T(8,128)(2,1)} %cot_ref.3), custom_call_target="tpu_custom_call" | custom-call | flops 1073741824 | bytes 10000000 | tf_op jit(solution)/shard_map/finish_out/pallas_call | solution.py:171
  215.4 24.8 %all-to-all-done.3.back_ref = bf16[128,8,2048]{2,1,0:T(8,128)(2,1)} async-done(((bf16[128,8,2048]{2,1,0:T(8,128)(2,1)}), bf16[128,8,2048]{2,1,0:T(8,128)(2,1)}, u32[]{:S(2)}, u32[]{:S(2)}) %all-to-all-start.3) | async-done | bytes 4194336 | tf_op jit(solution)/shard_map/all_to_all | solution.py:223
  240.1 3.5 %finish_in.1 = bf16[128,2048]{1,0:T(8,128)(2,1)} custom-call(bf16[128,8,2048]{2,1,0:T(8,128)(2,1)} %all-to-all-done.3.back_ref, bf16[128,1024]{1,0:T(8,128)(2,1)} %get-tuple-element.30.both_ref), custom_call_target="tpu_custom_call" | custom-call | tf_op jit(solution)/shard_map/finish_in/pallas_call | solution.py:204
  243.6 0.0 copy-done.1
Async XLA Ops:
  0.6 88.6 %copy-start = (bf16[1,704,2048]{2,1,0:T(8,128)(2,1)S(1)}, bf16[1,704,2048]{2,1,0:T(8,128)(2,1)}, u32[]{:S(2)}) copy-start(bf16[1,704,2048]{2,1,0:T(8,128)(2,1)} %param.15) | copy-start | bytes 8650756
  5.6 63.2 %all-to-all-start = ((bf16[128,8,2048]{2,1,0:T(8,128)(2,1)}), bf16[128,8,2048]{2,1,0:T(8,128)(2,1)}, u32[]{:S(2)}, u32[]{:S(2)}) async-start(bf16[128,8,2048]{2,1,0:T(8,128)(2,1)} %bitcast.64), calls=%async_computation | async-start | bytes 8388608 | tf_op jit(solution)/shard_map/all_to_all | solution.py:223
  68.8 57.1 %all-to-all-start.1 = ((bf16[128,8,2048]{2,1,0:T(8,128)(2,1)}), bf16[128,8,2048]{2,1,0:T(8,128)(2,1)}, u32[]{:S(2)}, u32[]{:S(2)}) async-start(bf16[128,8,2048]{2,1,0:T(8,128)(2,1)} %bitcast.61), calls=%async_computation.1 | async-start | bytes 8388608 | tf_op jit(solution)/shard_map/all_to_all | solution.py:223
  73.9 6.0 %copy-start.3 = (bf16[1,2048,704]{1,2,0:T(8,128)(2,1)S(1)}, bf16[1,2048,704]{1,2,0:T(8,128)(2,1)}, u32[]{:S(2)}) copy-start(bf16[1,2048,704]{1,2,0:T(8,128)(2,1)} %param.14) | copy-start | bytes 8650756
  80.0 8.1 %copy-start.7 = (f32[1024,704]{0,1:T(8,128)}, f32[1024,704]{0,1:T(8,128)S(1)}, u32[]{:S(2)}) copy-start(f32[1024,704]{0,1:T(8,128)S(1)} %fusion.6) | copy-start | bytes 8650756
  88.1 1.1 copy-start.10
  125.9 57.1 %all-to-all-start.2 = ((bf16[128,8,2048]{2,1,0:T(8,128)(2,1)}), bf16[128,8,2048]{2,1,0:T(8,128)(2,1)}, u32[]{:S(2)}, u32[]{:S(2)}) async-start(bf16[128,8,2048]{2,1,0:T(8,128)(2,1)} %bitcast.63), calls=%async_computation.2 | async-start | bytes 8388608 | tf_op jit(solution)/shard_map/all_to_all | solution.py:223
  131.1 7.4 %copy-start.2 = (bf16[1,2048,704]{1,2,0:T(8,128)(2,1)S(1)}, bf16[1,2048,704]{1,2,0:T(8,128)(2,1)}, u32[]{:S(2)}) copy-start(bf16[1,2048,704]{1,2,0:T(8,128)(2,1)} %param.13) | copy-start | bytes 8650756
  138.5 3.6 %copy-start.5 = (bf16[1024,704]{0,1:T(8,128)(2,1)}, bf16[1024,704]{0,1:T(8,128)(2,1)S(1)}, u32[]{:S(2)}) copy-start(bf16[1024,704]{0,1:T(8,128)(2,1)S(1)} %get-tuple-element.33) | copy-start | bytes 4325380
  138.5 3.6 %copy-start.8 = (bf16[1024,704]{0,1:T(8,128)(2,1)}, bf16[1024,704]{0,1:T(8,128)(2,1)S(1)}, u32[]{:S(2)}) copy-start(bf16[1024,704]{0,1:T(8,128)(2,1)S(1)} %get-tuple-element.32) | copy-start | bytes 4325380
  138.5 3.6 %copy-start.4 = (bf16[1,2048,704]{1,2,0:T(8,128)(2,1)S(1)}, bf16[1,2048,704]{1,2,0:T(8,128)(2,1)}, u32[]{:S(2)}) copy-start(bf16[1,2048,704]{1,2,0:T(8,128)(2,1)} %param.14) | copy-start | bytes 8650756
  183.0 7.0 %copy-start.11 = (bf16[1024,704]{0,1:T(8,128)(2,1)S(1)}, bf16[1024,704]{0,1:T(8,128)(2,1)}, u32[]{:S(2)}) copy-start(bf16[1024,704]{0,1:T(8,128)(2,1)} %copy-done.10) | copy-start | bytes 4325380
  183.0 57.1 %all-to-all-start.3 = ((bf16[128,8,2048]{2,1,0:T(8,128)(2,1)}), bf16[128,8,2048]{2,1,0:T(8,128)(2,1)}, u32[]{:S(2)}, u32[]{:S(2)}) async-start(bf16[128,8,2048]{2,1,0:T(8,128)(2,1)} %bitcast.62), calls=%async_computation.3 | async-start | bytes 8388608 | tf_op jit(solution)/shard_map/all_to_all | solution.py:223
  189.9 6.7 %copy-start.9 = (bf16[1024,704]{0,1:T(8,128)(2,1)S(1)}, bf16[1024,704]{0,1:T(8,128)(2,1)}, u32[]{:S(2)}) copy-start(bf16[1024,704]{0,1:T(8,128)(2,1)} %copy-done.8) | copy-start | bytes 4325380
  196.7 6.7 %copy-start.6 = (bf16[1024,704]{0,1:T(8,128)(2,1)S(1)}, bf16[1024,704]{0,1:T(8,128)(2,1)}, u32[]{:S(2)}) copy-start(bf16[1024,704]{0,1:T(8,128)(2,1)} %copy-done.5) | copy-start | bytes 4325380
  210.0 33.6 %copy-start.1 = (bf16[1,704,2048]{2,1,0:T(8,128)(2,1)S(1)}, bf16[1,704,2048]{2,1,0:T(8,128)(2,1)}, u32[]{:S(2)}) copy-start(bf16[1,704,2048]{2,1,0:T(8,128)(2,1)} %param.15) | copy-start | bytes 8650756

commit v3 on v2

--- a/solution.py
+++ b/solution.py
@@ -7,6 +7,7 @@
 
 AXES = ("dp", "expert")
 CAP = 8
+PARTS = 4
 VMEM_LIMIT = 60 * 1024 * 1024
 
 
@@ -20,84 +21,105 @@
     return jnp.sum(jnp.where(eye, column, 0.0), axis=0, keepdims=True)
 
 
-def prepare_kernel(coded_hbm, scale_ref, routes_ref, weight_ref, out_ref, pick_ref, slot_weight_ref, place_ref, coded_ref, inputs_ref, sem):
+def pick_rows(routes_ref, experts, tokens):
+    numbers = lax.broadcasted_iota(jnp.int32, (experts, tokens), 0)
+    first = routes_ref[0:1, :] == numbers
+    second = routes_ref[1:2, :] == numbers
+    named = jnp.where(first | second, 1.0, 0.0)
+    earlier = lax.broadcasted_iota(jnp.int32, (tokens, tokens), 0) < lax.broadcasted_iota(jnp.int32, (tokens, tokens), 1)
+    rank = jnp.dot(
+        named.astype(jnp.bfloat16),
+        jnp.where(earlier, 1.0, 0.0).astype(jnp.bfloat16),
+        preferred_element_type=jnp.float32,
+    )
+    slots = lax.broadcasted_iota(jnp.int32, (experts, CAP, tokens), 1).astype(jnp.float32)
+    slot_of = jnp.where(named > 0.0, rank, -1.0)
+    pick = jnp.broadcast_to(slot_of[:, None, :], (experts, CAP, tokens)) == slots
+    return pick, first, second, rank
+
+
+def as_matrix(pick):
+    experts, cap, tokens = pick.shape
+    return jnp.where(pick, 1.0, 0.0).astype(jnp.bfloat16).reshape(experts * cap, tokens)
+
+
+def send_in_kernel(coded_hbm, scale_ref, routes_ref, out_hbm, coded_ref, rows_ref, in_sem, out_sem):
     tokens, width = coded_ref.shape
     blocks = scale_ref.shape[0]
     size = width // blocks
-    experts = tokens // 2
-    part = out_ref.shape[0] * CAP
-    step = pl.program_id(0)
-
-    @pl.when(step == 0)
-    def _():
-        copy = pltpu.make_async_copy(coded_hbm, coded_ref, sem)
-        copy.start()
-        numbers = lax.broadcasted_iota(jnp.int32, (experts, tokens), 0)
-        first = routes_ref[0:1, :] == numbers
-        second = routes_ref[1:2, :] == numbers
-        named = jnp.where(first | second, 1.0, 0.0)
-        earlier = lax.broadcasted_iota(jnp.int32, (tokens, tokens), 0) < lax.broadcasted_iota(jnp.int32, (tokens, tokens), 1)
-        rank = jnp.dot(
-            named.astype(jnp.bfloat16),
-            jnp.where(earlier, 1.0, 0.0).astype(jnp.bfloat16),
-            preferred_element_type=jnp.float32,
-        )
-        weight = jnp.where(first, weight_ref[0:1, :], 0.0) + jnp.where(second, weight_ref[1:2, :], 0.0)
-        slots = lax.broadcasted_iota(jnp.int32, (experts, CAP, tokens), 1).astype(jnp.float32)
-        slot_of = jnp.where(named > 0.0, rank, -1.0)
-        pick = jnp.broadcast_to(slot_of[:, None, :], (experts, CAP, tokens)) == slots
-        pick_ref[...] = jnp.where(pick, 1.0, 0.0).astype(jnp.bfloat16).reshape(experts * CAP, tokens)
-        spread = jnp.broadcast_to(weight[:, None, :], (experts, CAP, tokens))
-        slot_weight_ref[...] = jnp.sum(jnp.where(pick, spread, 0.0).reshape(experts * CAP, tokens), axis=1, keepdims=True)
-        place = numbers.astype(jnp.float32) * (2 * CAP) + rank
-        place_ref[0:1, :] = jnp.sum(jnp.where(first, place, 0.0), axis=0, keepdims=True)
-        place_ref[1:2, :] = jnp.sum(jnp.where(second, place, 0.0), axis=0, keepdims=True)
+    part = width // PARTS
+    experts = tokens // 2
+    copies_in = []
+    for k in range(PARTS):
+        span = pl.ds(k * part, part)
+        copies_in.append(pltpu.make_async_copy(coded_hbm.at[:, span], coded_ref.at[:, span], in_sem.at[k]))
+        copies_in[k].start()
+    pick = as_matrix(pick_rows(routes_ref, experts, tokens)[0])
+    scales = [row_to_column(scale_ref[b : b + 1, :], tokens) for b in range(blocks)]
+    copies = []
+    for k in range(PARTS):
+        span = pl.ds(k * part, part)
+        copies_in[k].wait()
+        for b in range(k * part // size, (k + 1) * part // size):
+            columns = pl.ds(b * size, size)
+            coded_ref[:, columns] = (coded_ref[:, columns].astype(jnp.float32) * scales[b]).astype(jnp.bfloat16)
+        rows = jnp.dot(pick, coded_ref[:, span], preferred_element_type=jnp.float32)
+        rows_ref[:, :, span] = rows.astype(jnp.bfloat16).reshape(experts, CAP, part)
+        for half in range(2):
+            copy = pltpu.make_async_copy(rows_ref.at[:, :, span], out_hbm.at[:, half, :, span], out_sem.at[k, half])
+            copy.start()
+            copies.append(copy)
+    for copy in copies:
         copy.wait()
-        for b in range(blocks):
-            columns = pl.ds(b * size, size)
-            scale = row_to_column(scale_ref[b : b + 1, :], tokens)
-            inputs_ref[:, columns] = (coded_ref[:, columns].astype(jnp.float32) * scale).astype(jnp.bfloat16)
-
-    pick = pick_ref[pl.ds(pl.multiple_of(step * part, part), part), :]
-    rows = jnp.dot(pick, inputs_ref[...], preferred_element_type=jnp.float32).astype(jnp.bfloat16)
-    rows = rows.reshape(-1, CAP, width)
-    out_ref[:, 0] = rows
-    out_ref[:, 1] = rows
-
-
-def prepare(coded, scale, routes, weight, steps=2):
+
+
+def send_in(coded, scale, routes):
     tokens, width = coded.shape
     experts = tokens // 2
-    whole = lambda i: (0, 0)
-    return pl.pallas_call(
-        prepare_kernel,
-        grid=(steps,),
-        in_specs=[
-            pl.BlockSpec(memory_space=pl.ANY),
-            pl.BlockSpec(scale.shape, whole),
-            pl.BlockSpec(routes.shape, whole),
-            pl.BlockSpec(weight.shape, whole),
-        ],
-        out_specs=(
-            pl.BlockSpec((experts // steps, 2, CAP, width), lambda i: (i, 0, 0, 0)),
-            pl.BlockSpec((experts * CAP, tokens), whole),
-            pl.BlockSpec((experts * CAP, 1), whole),
-            pl.BlockSpec((2, tokens), whole),
-        ),
+    vmem = pl.BlockSpec(memory_space=pltpu.VMEM)
+    hbm = pl.BlockSpec(memory_space=pl.ANY)
+    return pl.pallas_call(
+        send_in_kernel,
+        in_specs=[hbm, vmem, vmem],
+        out_specs=hbm,
+        out_shape=jax.ShapeDtypeStruct((experts, 2, CAP, width), jnp.bfloat16),
+        scratch_shapes=[
+            pltpu.VMEM((tokens, width), jnp.bfloat16),
+            pltpu.VMEM((experts, CAP, width), jnp.bfloat16),
+            pltpu.SemaphoreType.DMA((PARTS,)),
+            pltpu.SemaphoreType.DMA((PARTS, 2)),
+        ],
+        compiler_params=pltpu.CompilerParams(vmem_limit_bytes=VMEM_LIMIT),
+        name="send_in",
+    )(coded, scale, routes)
+
+
+def plan_kernel(routes_ref, weight_ref, pick_ref, slot_weight_ref, place_ref):
+    tokens = routes_ref.shape[1]
+    experts = tokens // 2
+    pick, first, second, rank = pick_rows(routes_ref, experts, tokens)
+    pick_ref[...] = as_matrix(pick)
+    weight = jnp.where(first, weight_ref[0:1, :], 0.0) + jnp.where(second, weight_ref[1:2, :], 0.0)
+    spread = jnp.broadcast_to(weight[:, None, :], pick.shape)
+    slot_weight_ref[...] = jnp.sum(jnp.where(pick, spread, 0.0).reshape(experts * CAP, tokens), axis=1, keepdims=True)
+    place = lax.broadcasted_iota(jnp.int32, (experts, tokens), 0).astype(jnp.float32) * (2 * CAP) + rank
+    place_ref[0:1, :] = jnp.sum(jnp.where(first, place, 0.0), axis=0, keepdims=True)
+    place_ref[1:2, :] = jnp.sum(jnp.where(second, place, 0.0), axis=0, keepdims=True)
+
+
+def plan(routes, weight):
+    tokens = routes.shape[1]
+    experts = tokens // 2
+    return pl.pallas_call(
+        plan_kernel,
         out_shape=(
-            jax.ShapeDtypeStruct((experts, 2, CAP, width), jnp.bfloat16),
             jax.ShapeDtypeStruct((experts * CAP, tokens), jnp.bfloat16),
             jax.ShapeDtypeStruct((experts * CAP, 1), jnp.float32),
             jax.ShapeDtypeStruct((2, tokens), jnp.float32),
         ),
-        scratch_shapes=[
-            pltpu.VMEM((tokens, width), jnp.bfloat16),
-            pltpu.VMEM((tokens, width), jnp.bfloat16),
-            pltpu.SemaphoreType.DMA(()),
-        ],
-        compiler_params=pltpu.CompilerParams(vmem_limit_bytes=VMEM_LIMIT),
-        name="prepare",
-    )(coded, scale, routes, weight)
+        compiler_params=pltpu.CompilerParams(vmem_limit_bytes=VMEM_LIMIT),
+        name="plan",
+    )(routes, weight)
 
 
 def select_kernel(place_ref, first_ref, second_ref, both_ref):
@@ -229,9 +251,12 @@
     weight = route_weight.T
     gate_w, up_w, down_w = w_gate[0].T, w_up[0].T, w_down[0]
 
-    send_rows, pick, slot_weight, place = prepare(coded, block_scale.T, routes.T, weight)
+    send_rows = send_in(coded, block_scale.T, routes.T)
     rows = exchange(send_rows.reshape(nodes, CAP, width))
-    cot_rows = exchange(send_cot(cotangent, pick, slot_weight).reshape(nodes, CAP, width))
+    late_routes, _ = lax.optimization_barrier((routes.T, send_rows))
+    pick, slot_weight, place = plan(late_routes, weight)
+    rows, send_cots = lax.optimization_barrier((rows, send_cot(cotangent, pick, slot_weight)))
+    cot_rows = exchange(send_cots.reshape(nodes, CAP, width))
     rows = rows.reshape(-1, width)
     cot_rows = cot_rows.reshape(-1, width)
 

time: 244 us -> 244 us (level)
    pallas_call x1 -> x2, Pallas kernels: 4.92 us -> 5.98 us  [the longest x1 4.28 us: send_in(): pl.pallas_call(send_in_kernel, in_specs=[hbm, vmem, vmem], out_specs=hbm,...]
  transfers between devices with their start and end apart: 4 -> 4, of which waited for: 4 -> 4; matrix products, arithmetic and copies ran while one was open for 23% -> 23% of each run, Pallas kernels for 5% -> 6%
where the time goes in v3:
time: 244 us; the launch traced here: 243 us
  waiting for transfers between devices  137 us (56%)
  matrix products  55.6 us (23%)
  starting transfers between devices  26.8 us (11%)
  Pallas kernels  21.1 us (9%)
    all_to_all x4, waiting for transfers between devices, exchange(): return lax.all_to_all(rows, AXES, split_axis=0, concat_axis=0, tiled=True)  137 us
    dot_general x9, matrix products, dot(): lax.dot_general(a, b, (((a_dim,), (b_dim,)), ((), ())), preferred_element...  55.6 us
    all_to_all x4, starting transfers between devices, exchange(): return lax.all_to_all(rows, AXES, split_axis=0, concat_axis=0, tiled=True)  26.8 us
    pallas_call x1, Pallas kernels, finish_out(): pl.pallas_call(finish_out_kernel, grid=(steps,), in_specs=[pl.BlockSpec((...  5.35 us
  transfers between devices with their start and end apart: 4, of which 4 were waited for; matrix products, arithmetic and copies ran while one was open for 23% of the time, Pallas kernels for 6%

profile of v3, /device:TPU:7, one launch (start us, length us, event | category | flops | bytes accessed | tf_op | source)
XLA Modules:
  0.0 243.0 jit_solution(15465032633281713810)
XLA Ops:
  0.6 0.0 copy-start
  0.6 4.3 %send_in.1 = bf16[64,2,8,2048]{3,2,1,0:T(8,128)(2,1)} custom-call(bf16[128,2048]{1,0:T(8,128)(2,1)} %coded_hbm.1, f32[16,128]{1,0:T(8,128)} %bitcast.65, s32[2,128]{1,0:T(2,128)} %bitcast.66), custom_call_target="tpu_custom_call" | custom-call | tf_op jit(solution)/shard_map/send_in/pallas_call | solution.py:81
  4.9 11.3 %all-to-all-start = ((bf16[128,8,2048]{2,1,0:T(8,128)(2,1)}), bf16[128,8,2048]{2,1,0:T(8,128)(2,1)}, u32[]{:S(2)}, u32[]{:S(2)}) async-start(bf16[128,8,2048]{2,1,0:T(8,128)(2,1)} %bitcast.62), calls=%async_computation | async-start | bytes 8388608 | tf_op jit(solution)/shard_map/all_to_all | solution.py:245
  16.2 1.7 plan.1
  17.9 4.6 %send_cot.1 = bf16[64,2,8,2048]{3,2,1,0:T(8,128)(2,1)} custom-call(bf16[128,2048]{1,0:T(8,128)(2,1)} %cot_ref.3, bf16[512,128]{1,0:T(8,128)(2,1)} %get-tuple-element.22.pick_ref, f32[512,1]{1,0:T(8,128)} %get-tuple-element.23.weight_ref), custom_call_target="tpu_custom_call" | custom-call | flops 268435456 | bytes 10000000 | tf_op jit(solution)/shard_map/send_cot/pallas_call | solution.py:153
  22.5 45.6 %all-to-all-done = bf16[128,8,2048]{2,1,0:T(8,128)(2,1)} async-done(((bf16[128,8,2048]{2,1,0:T(8,128)(2,1)}), bf16[128,8,2048]{2,1,0:T(8,128)(2,1)}, u32[]{:S(2)}, u32[]{:S(2)}) %all-to-all-start) | async-done | bytes 4194336 | tf_op jit(solution)/shard_map/all_to_all | solution.py:245
  68.1 5.2 %all-to-all-start.1 = ((bf16[128,8,2048]{2,1,0:T(8,128)(2,1)}), bf16[128,8,2048]{2,1,0:T(8,128)(2,1)}, u32[]{:S(2)}, u32[]{:S(2)}) async-start(bf16[128,8,2048]{2,1,0:T(8,128)(2,1)} %bitcast.61), calls=%async_computation.1 | async-start | bytes 8388608 | tf_op jit(solution)/shard_map/all_to_all | solution.py:245
  73.3 0.0 copy-start.3
  73.3 6.0 %fusion.6 = f32[1024,704]{0,1:T(8,128)S(1)} fusion(bf16[128,8,2048]{2,1,0:T(8,128)(2,1)} %all-to-all-done, bf16[1,2048,704]{1,2,0:T(8,128)(2,1)} %param.13), kind=kOutput, calls=%fused_computation.7 | convolution fusion | flops 2952790016 | bytes 9961472 | tf_op jit(solution)/shard_map/dot_general | solution.py:241
  79.3 0.0 copy-done.3
  79.4 0.0 copy-start.7
  79.4 8.1 %multiply_convert_fusion.2 = (bf16[1024,704]{0,1:T(8,128)(2,1)S(1)}, f32[1024,704]{0,1:T(8,128)}) fusion(f32[1024,704]{0,1:T(8,128)S(1)} %fusion.6, bf16[1,2048,704]{1,2,0:T(8,128)(2,1)S(1)} %copy-done.3, bf16[128,8,2048]{2,1,0:T(8,128)(2,1)} %all-to-all-done), kind=kOutput, calls=%fused_computation.26 | convolution fusion | flops 2957115392 | bytes 14286848 | tf_op jit(solution)/shard_map/dot_general | solution.py:241
  87.5 0.0 copy-done.7
  87.5 0.0 copy-start.10
  87.5 1.1 copy-done.10
  88.6 0.0 copy-done
  88.6 5.0 %convolution_convert_fusion = bf16[1024,2048]{1,0:T(8,128)(2,1)} fusion(bf16[1024,704]{0,1:T(8,128)(2,1)S(1)} %get-tuple-element.38, bf16[1,704,2048]{2,1,0:T(8,128)(2,1)S(1)} %copy-done), kind=kOutput, calls=%fused_computation.9 | convolution fusion | flops 2954887168 | bytes 8519680 | tf_op jit(solution)/shard_map/dot_general | solution.py:241
  93.6 31.6 %all-to-all-done.1 = bf16[128,8,2048]{2,1,0:T(8,128)(2,1)} async-done(((bf16[128,8,2048]{2,1,0:T(8,128)(2,1)}), bf16[128,8,2048]{2,1,0:T(8,128)(2,1)}, u32[]{:S(2)}, u32[]{:S(2)}) %all-to-all-start.1) | async-done | bytes 4194336 | tf_op jit(solution)/shard_map/all_to_all | solution.py:245
  125.2 5.2 %all-to-all-start.2 = ((bf16[128,8,2048]{2,1,0:T(8,128)(2,1)}), bf16[128,8,2048]{2,1,0:T(8,128)(2,1)}, u32[]{:S(2)}, u32[]{:S(2)}) async-start(bf16[128,8,2048]{2,1,0:T(8,128)(2,1)} %bitcast.64), calls=%async_computation.2 | async-start | bytes 8388608 | tf_op jit(solution)/shard_map/all_to_all | solution.py:245
  130.4 0.0 copy-start.2
  130.5 7.4 %multiply_convert_fusion = (bf16[1024,704]{0,1:T(8,128)(2,1)S(1)}, bf16[1024,704]{0,1:T(8,128)(2,1)S(1)}) fusion(f32[1024,704]{0,1:T(8,128)} %copy-done.7, f32[1024,704]{0,1:T(8,128)} %get-tuple-element.39, bf16[1024,2048]{1,0:T(8,128)(2,1)} %bitcast.9, bf16[1,704,2048]{2,1,0:T(8,128)(2,1)S(1)} %copy-done), kind=kOutput, calls=%fused_computation.24 | convolution fusion | flops 2962161664 | bytes 15728640 | tf_op jit(solution)/shard_map/dot_general | solution.py:241
  137.8 0.0 copy-start.5
  137.9 0.0 copy-start.8
  137.9 0.0 copy-done.2
  137.9 0.0 copy-start.4
  137.9 3.5 %fusion.26 = f32[1024,2048]{1,0:T(8,128)S(1)} fusion(bf16[1024,704]{0,1:T(8,128)(2,1)S(1)} %get-tuple-element.37, bf16[1,2048,704]{1,2,0:T(8,128)(2,1)S(1)} %copy-done.2), kind=kOutput, calls=%fused_computation.21 | convolution fusion | flops 2952790016 | bytes 12713984 | tf_op jit(solution)/shard_map/dot_general | solution.py:241
  141.4 0.0 copy-done.5
  141.4 0.0 copy-done.8
  141.5 0.0 copy-done.4
  141.5 5.5 %add_convert_fusion = bf16[1024,2048]{1,0:T(8,128)(2,1)} fusion(f32[1024,2048]{1,0:T(8,128)S(1)} %fusion.26, bf16[1024,704]{0,1:T(8,128)(2,1)S(1)} %get-tuple-element.36, bf16[1,2048,704]{1,2,0:T(8,128)(2,1)S(1)} %copy-done.4), kind=kOutput, calls=%fused_computation | convolution fusion | flops 2956984320 | bytes 16908288 | tf_op jit(solution)/shard_map/dot_general | solution.py:241
  146.9 35.4 %all-to-all-done.2.back_ref = bf16[128,8,2048]{2,1,0:T(8,128)(2,1)} async-done(((bf16[128,8,2048]{2,1,0:T(8,128)(2,1)}), bf16[128,8,2048]{2,1,0:T(8,128)(2,1)}, u32[]{:S(2)}, u32[]{:S(2)}) %all-to-all-start.2) | async-done | bytes 4194336 | tf_op jit(solution)/shard_map/all_to_all | solution.py:245
  182.4 0.0 copy-start.11
  182.4 5.2 %all-to-all-start.3 = ((bf16[128,8,2048]{2,1,0:T(8,128)(2,1)}), bf16[128,8,2048]{2,1,0:T(8,128)(2,1)}, u32[]{:S(2)}, u32[]{:S(2)}) async-start(bf16[128,8,2048]{2,1,0:T(8,128)(2,1)} %bitcast.63), calls=%async_computation.3 | async-start | bytes 8388608 | tf_op jit(solution)/shard_map/all_to_all | solution.py:245
  187.6 1.8 select.1
  189.3 0.0 copy-done.11
  189.3 0.0 copy-start.6
  189.3 6.7 %fusion.14 = bf16[1,704,2048]{2,1,0:T(8,128)(2,1)} fusion(bf16[1024,704]{0,1:T(8,128)(2,1)S(1)} %copy-done.11, bf16[1024,2048]{1,0:T(8,128)(2,1)} %bitcast.9), kind=kOutput, calls=%fused_computation.13 | convolution fusion | flops 2954231808 | bytes 8519680 | tf_op jit(solution)/shard_map/dot_general | solution.py:241
  196.0 0.0 copy-done.6
  196.0 0.0 copy-start.9
  196.0 6.7 %fusion.15 = bf16[1,2048,704]{1,2,0:T(8,128)(2,1)} fusion(bf16[1024,704]{0,1:T(8,128)(2,1)S(1)} %copy-done.6, bf16[128,8,2048]{2,1,0:T(8,128)(2,1)} %all-to-all-done), kind=kOutput, calls=%fused_computation.14 | convolution fusion | flops 2954231808 | bytes 8519680 | tf_op jit(solution)/shard_map/dot_general | solution.py:241
  202.8 0.0 copy-done.9
  202.8 6.6 %fusion.18 = bf16[1,2048,704]{1,2,0:T(8,128)(2,1)} fusion(bf16[1024,704]{0,1:T(8,128)(2,1)S(1)} %copy-done.9, bf16[128,8,2048]{2,1,0:T(8,128)(2,1)} %all-to-all-done), kind=kOutput, calls=%fused_computation.15 | convolution fusion | flops 2954231808 | bytes 8519680 | tf_op jit(solution)/shard_map/dot_general | solution.py:241
  209.4 0.0 copy-start.1
  209.4 5.4 %finish_out.1 = (bf16[128,2048]{1,0:T(8,128)(2,1)}, f32[2,128]{1,0:T(2,128)}) custom-call(bf16[128,8,2048]{2,1,0:T(8,128)(2,1)} %all-to-all-done.2.back_ref, bf16[128,1024]{1,0:T(8,128)(2,1)} %get-tuple-element.30.first_ref, bf16[128,1024]{1,0:T(8,128)(2,1)} %get-tuple-element.31.second_ref, f32[2,128]{1,0:T(2,128)} %bitcast.69, bf16[128,2048]{1,0:T(8,128)(2,1)} %cot_ref.3), custom_call_target="tpu_custom_call" | custom-call | flops 1073741824 | bytes 10000000 | tf_op jit(solution)/shard_map/finish_out/pallas_call | solution.py:193
  214.7 24.8 %all-to-all-done.3.back_ref = bf16[128,8,2048]{2,1,0:T(8,128)(2,1)} async-done(((bf16[128,8,2048]{2,1,0:T(8,128)(2,1)}), bf16[128,8,2048]{2,1,0:T(8,128)(2,1)}, u32[]{:S(2)}, u32[]{:S(2)}) %all-to-all-start.3) | async-done | bytes 4194336 | tf_op jit(solution)/shard_map/all_to_all | solution.py:245
  239.5 3.5 %finish_in.1 = bf16[128,2048]{1,0:T(8,128)(2,1)} custom-call(bf16[128,8,2048]{2,1,0:T(8,128)(2,1)} %all-to-all-done.3.back_ref, bf16[128,1024]{1,0:T(8,128)(2,1)} %get-tuple-element.34.both_ref), custom_call_target="tpu_custom_call" | custom-call | tf_op jit(solution)/shard_map/finish_in/pallas_call | solution.py:226
  243.0 0.0 copy-done.1
Async XLA Ops:
  0.6 88.0 %copy-start = (bf16[1,704,2048]{2,1,0:T(8,128)(2,1)S(1)}, bf16[1,704,2048]{2,1,0:T(8,128)(2,1)}, u32[]{:S(2)}) copy-start(bf16[1,704,2048]{2,1,0:T(8,128)(2,1)} %param.15) | copy-start | bytes 8650756
  4.9 63.2 %all-to-all-start = ((bf16[128,8,2048]{2,1,0:T(8,128)(2,1)}), bf16[128,8,2048]{2,1,0:T(8,128)(2,1)}, u32[]{:S(2)}, u32[]{:S(2)}) async-start(bf16[128,8,2048]{2,1,0:T(8,128)(2,1)} %bitcast.62), calls=%async_computation | async-start | bytes 8388608 | tf_op jit(solution)/shard_map/all_to_all | solution.py:245
  68.1 57.1 %all-to-all-start.1 = ((bf16[128,8,2048]{2,1,0:T(8,128)(2,1)}), bf16[128,8,2048]{2,1,0:T(8,128)(2,1)}, u32[]{:S(2)}, u32[]{:S(2)}) async-start(bf16[128,8,2048]{2,1,0:T(8,128)(2,1)} %bitcast.61), calls=%async_computation.1 | async-start | bytes 8388608 | tf_op jit(solution)/shard_map/all_to_all | solution.py:245
  73.3 6.0 %copy-start.3 = (bf16[1,2048,704]{1,2,0:T(8,128)(2,1)S(1)}, bf16[1,2048,704]{1,2,0:T(8,128)(2,1)}, u32[]{:S(2)}) copy-start(bf16[1,2048,704]{1,2,0:T(8,128)(2,1)} %param.14) | copy-start | bytes 8650756
  79.4 8.1 %copy-start.7 = (f32[1024,704]{0,1:T(8,128)}, f32[1024,704]{0,1:T(8,128)S(1)}, u32[]{:S(2)}) copy-start(f32[1024,704]{0,1:T(8,128)S(1)} %fusion.6) | copy-start | bytes 8650756
  87.5 1.1 copy-start.10
  125.2 57.1 %all-to-all-start.2 = ((bf16[128,8,2048]{2,1,0:T(8,128)(2,1)}), bf16[128,8,2048]{2,1,0:T(8,128)(2,1)}, u32[]{:S(2)}, u32[]{:S(2)}) async-start(bf16[128,8,2048]{2,1,0:T(8,128)(2,1)} %bitcast.64), calls=%async_computation.2 | async-start | bytes 8388608 | tf_op jit(solution)/shard_map/all_to_all | solution.py:245
  130.4 7.4 %copy-start.2 = (bf16[1,2048,704]{1,2,0:T(8,128)(2,1)S(1)}, bf16[1,2048,704]{1,2,0:T(8,128)(2,1)}, u32[]{:S(2)}) copy-start(bf16[1,2048,704]{1,2,0:T(8,128)(2,1)} %param.13) | copy-start | bytes 8650756
  137.8 3.6 %copy-start.5 = (bf16[1024,704]{0,1:T(8,128)(2,1)}, bf16[1024,704]{0,1:T(8,128)(2,1)S(1)}, u32[]{:S(2)}) copy-start(bf16[1024,704]{0,1:T(8,128)(2,1)S(1)} %get-tuple-element.37) | copy-start | bytes 4325380
  137.9 3.6 %copy-start.8 = (bf16[1024,704]{0,1:T(8,128)(2,1)}, bf16[1024,704]{0,1:T(8,128)(2,1)S(1)}, u32[]{:S(2)}) copy-start(bf16[1024,704]{0,1:T(8,128)(2,1)S(1)} %get-tuple-element.36) | copy-start | bytes 4325380
  137.9 3.6 %copy-start.4 = (bf16[1,2048,704]{1,2,0:T(8,128)(2,1)S(1)}, bf16[1,2048,704]{1,2,0:T(8,128)(2,1)}, u32[]{:S(2)}) copy-start(bf16[1,2048,704]{1,2,0:T(8,128)(2,1)} %param.14) | copy-start | bytes 8650756
  182.4 7.0 %copy-start.11 = (bf16[1024,704]{0,1:T(8,128)(2,1)S(1)}, bf16[1024,704]{0,1:T(8,128)(2,1)}, u32[]{:S(2)}) copy-start(bf16[1024,704]{0,1:T(8,128)(2,1)} %copy-done.10) | copy-start | bytes 4325380
  182.4 57.1 %all-to-all-start.3 = ((bf16[128,8,2048]{2,1,0:T(8,128)(2,1)}), bf16[128,8,2048]{2,1,0:T(8,128)(2,1)}, u32[]{:S(2)}, u32[]{:S(2)}) async-start(bf16[128,8,2048]{2,1,0:T(8,128)(2,1)} %bitcast.63), calls=%async_computation.3 | async-start | bytes 8388608 | tf_op jit(solution)/shard_map/all_to_all | solution.py:245
  189.3 6.7 %copy-start.6 = (bf16[1024,704]{0,1:T(8,128)(2,1)S(1)}, bf16[1024,704]{0,1:T(8,128)(2,1)}, u32[]{:S(2)}) copy-start(bf16[1024,704]{0,1:T(8,128)(2,1)} %copy-done.5) | copy-start | bytes 4325380
  196.0 6.7 %copy-start.9 = (bf16[1024,704]{0,1:T(8,128)(2,1)S(1)}, bf16[1024,704]{0,1:T(8,128)(2,1)}, u32[]{:S(2)}) copy-start(bf16[1024,704]{0,1:T(8,128)(2,1)} %copy-done.8) | copy-start | bytes 4325380
  209.4 33.6 %copy-start.1 = (bf16[1,704,2048]{2,1,0:T(8,128)(2,1)S(1)}, bf16[1,704,2048]{2,1,0:T(8,128)(2,1)}, u32[]{:S(2)}) copy-start(bf16[1,704,2048]{2,1,0:T(8,128)(2,1)} %param.15) | copy-start | bytes 8650756

commit v4 on v3

--- a/solution.py
+++ b/solution.py
@@ -43,23 +43,26 @@
     return jnp.where(pick, 1.0, 0.0).astype(jnp.bfloat16).reshape(experts * cap, tokens)
 
 
-def send_in_kernel(coded_hbm, scale_ref, routes_ref, out_hbm, coded_ref, rows_ref, in_sem, out_sem):
+def send_in_kernel(coded_hbm, scale_hbm, routes_hbm, out_hbm, coded_ref, rows_ref, scale_ref, routes_ref, in_sem, out_sem):
     tokens, width = coded_ref.shape
     blocks = scale_ref.shape[0]
     size = width // blocks
     part = width // PARTS
     experts = tokens // 2
-    copies_in = []
-    for k in range(PARTS):
-        span = pl.ds(k * part, part)
-        copies_in.append(pltpu.make_async_copy(coded_hbm.at[:, span], coded_ref.at[:, span], in_sem.at[k]))
-        copies_in[k].start()
+    copy_routes = pltpu.make_async_copy(routes_hbm, routes_ref, in_sem.at[0])
+    copy_routes.start()
+    copy_scale = pltpu.make_async_copy(scale_hbm, scale_ref, in_sem.at[1])
+    copy_scale.start()
+    copy_coded = pltpu.make_async_copy(coded_hbm, coded_ref, in_sem.at[2])
+    copy_coded.start()
+    copy_routes.wait()
     pick = as_matrix(pick_rows(routes_ref, experts, tokens)[0])
+    copy_scale.wait()
     scales = [row_to_column(scale_ref[b : b + 1, :], tokens) for b in range(blocks)]
+    copy_coded.wait()
     copies = []
     for k in range(PARTS):
         span = pl.ds(k * part, part)
-        copies_in[k].wait()
         for b in range(k * part // size, (k + 1) * part // size):
             columns = pl.ds(b * size, size)
             coded_ref[:, columns] = (coded_ref[:, columns].astype(jnp.float32) * scales[b]).astype(jnp.bfloat16)
@@ -76,17 +79,18 @@
 def send_in(coded, scale, routes):
     tokens, width = coded.shape
     experts = tokens // 2
-    vmem = pl.BlockSpec(memory_space=pltpu.VMEM)
     hbm = pl.BlockSpec(memory_space=pl.ANY)
     return pl.pallas_call(
         send_in_kernel,
-        in_specs=[hbm, vmem, vmem],
+        in_specs=[hbm, hbm, hbm],
         out_specs=hbm,
         out_shape=jax.ShapeDtypeStruct((experts, 2, CAP, width), jnp.bfloat16),
         scratch_shapes=[
             pltpu.VMEM((tokens, width), jnp.bfloat16),
             pltpu.VMEM((experts, CAP, width), jnp.bfloat16),
-            pltpu.SemaphoreType.DMA((PARTS,)),
+            pltpu.VMEM(scale.shape, jnp.float32),
+            pltpu.VMEM(routes.shape, jnp.int32),
+            pltpu.SemaphoreType.DMA((3,)),
             pltpu.SemaphoreType.DMA((PARTS, 2)),
         ],
         compiler_params=pltpu.CompilerParams(vmem_limit_bytes=VMEM_LIMIT),

time: 244 us -> 243 us (level)
  no operation moved by 1% of the time
where the time goes in v4:
time: 243 us
  waiting for transfers between devices  137 us (56%)
  matrix products  55.6 us (23%)
  starting transfers between devices  26.8 us (11%)
  Pallas kernels  20.7 us (9%)
    all_to_all x4, waiting for transfers between devices, exchange(): return lax.all_to_all(rows, AXES, split_axis=0, concat_axis=0, tiled=True)  137 us
    dot_general x9, matrix products, dot(): lax.dot_general(a, b, (((a_dim,), (b_dim,)), ((), ())), preferred_element...  55.6 us
    all_to_all x4, starting transfers between devices, exchange(): return lax.all_to_all(rows, AXES, split_axis=0, concat_axis=0, tiled=True)  26.8 us
    pallas_call x1, Pallas kernels, finish_out(): pl.pallas_call(finish_out_kernel, grid=(steps,), in_specs=[pl.BlockSpec((...  5.35 us
  transfers between devices with their start and end apart: 4, of which 4 were waited for; matrix products, arithmetic and copies ran while one was open for 23% of the time, Pallas kernels for 6%

profile of v4, /device:TPU:7, one launch (start us, length us, event | category | flops | bytes accessed | tf_op | source)
XLA Modules:
  0.0 242.5 jit_solution(8116532101452424230)
XLA Ops:
  0.6 0.0 copy-start
  0.6 3.9 %send_in.1 = bf16[64,2,8,2048]{3,2,1,0:T(8,128)(2,1)} custom-call(bf16[128,2048]{1,0:T(8,128)(2,1)} %coded_hbm.1, f32[16,128]{1,0:T(8,128)} %bitcast.65, s32[2,128]{1,0:T(2,128)} %bitcast.66), custom_call_target="tpu_custom_call" | custom-call | tf_op jit(solution)/shard_map/send_in/pallas_call | solution.py:83
  4.5 11.3 %all-to-all-start = ((bf16[128,8,2048]{2,1,0:T(8,128)(2,1)}), bf16[128,8,2048]{2,1,0:T(8,128)(2,1)}, u32[]{:S(2)}, u32[]{:S(2)}) async-start(bf16[128,8,2048]{2,1,0:T(8,128)(2,1)} %bitcast.62), calls=%async_computation | async-start | bytes 8388608 | tf_op jit(solution)/shard_map/all_to_all | solution.py:249
  15.8 1.7 plan.1
  17.5 4.6 %send_cot.1 = bf16[64,2,8,2048]{3,2,1,0:T(8,128)(2,1)} custom-call(bf16[128,2048]{1,0:T(8,128)(2,1)} %cot_ref.3, bf16[512,128]{1,0:T(8,128)(2,1)} %get-tuple-element.22.pick_ref, f32[512,1]{1,0:T(8,128)} %get-tuple-element.23.weight_ref), custom_call_target="tpu_custom_call" | custom-call | flops 268435456 | bytes 10000000 | tf_op jit(solution)/shard_map/send_cot/pallas_call | solution.py:157
  22.1 45.6 %all-to-all-done = bf16[128,8,2048]{2,1,0:T(8,128)(2,1)} async-done(((bf16[128,8,2048]{2,1,0:T(8,128)(2,1)}), bf16[128,8,2048]{2,1,0:T(8,128)(2,1)}, u32[]{:S(2)}, u32[]{:S(2)}) %all-to-all-start) | async-done | bytes 4194336 | tf_op jit(solution)/shard_map/all_to_all | solution.py:249
  67.7 5.2 %all-to-all-start.1 = ((bf16[128,8,2048]{2,1,0:T(8,128)(2,1)}), bf16[128,8,2048]{2,1,0:T(8,128)(2,1)}, u32[]{:S(2)}, u32[]{:S(2)}) async-start(bf16[128,8,2048]{2,1,0:T(8,128)(2,1)} %bitcast.61), calls=%async_computation.1 | async-start | bytes 8388608 | tf_op jit(solution)/shard_map/all_to_all | solution.py:249
  72.9 0.0 copy-start.3
  72.9 6.0 %fusion.6 = f32[1024,704]{0,1:T(8,128)S(1)} fusion(bf16[128,8,2048]{2,1,0:T(8,128)(2,1)} %all-to-all-done, bf16[1,2048,704]{1,2,0:T(8,128)(2,1)} %param.13), kind=kOutput, calls=%fused_computation.7 | convolution fusion | flops 2952790016 | bytes 9961472 | tf_op jit(solution)/shard_map/dot_general | solution.py:245
  78.9 0.0 copy-done.3
  78.9 0.0 copy-start.7
  78.9 8.1 %multiply_convert_fusion.2 = (bf16[1024,704]{0,1:T(8,128)(2,1)S(1)}, f32[1024,704]{0,1:T(8,128)}) fusion(f32[1024,704]{0,1:T(8,128)S(1)} %fusion.6, bf16[1,2048,704]{1,2,0:T(8,128)(2,1)S(1)} %copy-done.3, bf16[128,8,2048]{2,1,0:T(8,128)(2,1)} %all-to-all-done), kind=kOutput, calls=%fused_computation.26 | convolution fusion | flops 2957115392 | bytes 14286848 | tf_op jit(solution)/shard_map/dot_general | solution.py:245
  87.0 0.0 copy-done.7
  87.0 0.0 copy-start.10
  87.1 1.1 copy-done.10
  88.1 0.0 copy-done
  88.2 5.0 %convolution_convert_fusion = bf16[1024,2048]{1,0:T(8,128)(2,1)} fusion(bf16[1024,704]{0,1:T(8,128)(2,1)S(1)} %get-tuple-element.38, bf16[1,704,2048]{2,1,0:T(8,128)(2,1)S(1)} %copy-done), kind=kOutput, calls=%fused_computation.9 | convolution fusion | flops 2954887168 | bytes 8519680 | tf_op jit(solution)/shard_map/dot_general | solution.py:245
  93.2 31.6 %all-to-all-done.1 = bf16[128,8,2048]{2,1,0:T(8,128)(2,1)} async-done(((bf16[128,8,2048]{2,1,0:T(8,128)(2,1)}), bf16[128,8,2048]{2,1,0:T(8,128)(2,1)}, u32[]{:S(2)}, u32[]{:S(2)}) %all-to-all-start.1) | async-done | bytes 4194336 | tf_op jit(solution)/shard_map/all_to_all | solution.py:249
  124.8 5.2 %all-to-all-start.2 = ((bf16[128,8,2048]{2,1,0:T(8,128)(2,1)}), bf16[128,8,2048]{2,1,0:T(8,128)(2,1)}, u32[]{:S(2)}, u32[]{:S(2)}) async-start(bf16[128,8,2048]{2,1,0:T(8,128)(2,1)} %bitcast.64), calls=%async_computation.2 | async-start | bytes 8388608 | tf_op jit(solution)/shard_map/all_to_all | solution.py:249
  130.0 0.0 copy-start.2
  130.0 7.4 %multiply_convert_fusion = (bf16[1024,704]{0,1:T(8,128)(2,1)S(1)}, bf16[1024,704]{0,1:T(8,128)(2,1)S(1)}) fusion(f32[1024,704]{0,1:T(8,128)} %copy-done.7, f32[1024,704]{0,1:T(8,128)} %get-tuple-element.39, bf16[1024,2048]{1,0:T(8,128)(2,1)} %bitcast.9, bf16[1,704,2048]{2,1,0:T(8,128)(2,1)S(1)} %copy-done), kind=kOutput, calls=%fused_computation.24 | convolution fusion | flops 2962161664 | bytes 15728640 | tf_op jit(solution)/shard_map/dot_general | solution.py:245
  137.4 0.0 copy-start.5
  137.4 0.0 copy-start.8
  137.4 0.0 copy-done.2
  137.5 0.0 copy-start.4
  137.5 3.5 %fusion.26 = f32[1024,2048]{1,0:T(8,128)S(1)} fusion(bf16[1024,704]{0,1:T(8,128)(2,1)S(1)} %get-tuple-element.37, bf16[1,2048,704]{1,2,0:T(8,128)(2,1)S(1)} %copy-done.2), kind=kOutput, calls=%fused_computation.21 | convolution fusion | flops 2952790016 | bytes 12713984 | tf_op jit(solution)/shard_map/dot_general | solution.py:245
  141.0 0.0 copy-done.5
  141.0 0.0 copy-done.8
  141.0 0.0 copy-done.4
  141.0 5.5 %add_convert_fusion = bf16[1024,2048]{1,0:T(8,128)(2,1)} fusion(f32[1024,2048]{1,0:T(8,128)S(1)} %fusion.26, bf16[1024,704]{0,1:T(8,128)(2,1)S(1)} %get-tuple-element.36, bf16[1,2048,704]{1,2,0:T(8,128)(2,1)S(1)} %copy-done.4), kind=kOutput, calls=%fused_computation | convolution fusion | flops 2956984320 | bytes 16908288 | tf_op jit(solution)/shard_map/dot_general | solution.py:245
  146.5 35.4 %all-to-all-done.2.back_ref = bf16[128,8,2048]{2,1,0:T(8,128)(2,1)} async-done(((bf16[128,8,2048]{2,1,0:T(8,128)(2,1)}), bf16[128,8,2048]{2,1,0:T(8,128)(2,1)}, u32[]{:S(2)}, u32[]{:S(2)}) %all-to-all-start.2) | async-done | bytes 4194336 | tf_op jit(solution)/shard_map/all_to_all | solution.py:249
  181.9 0.0 copy-start.11
  181.9 5.2 %all-to-all-start.3 = ((bf16[128,8,2048]{2,1,0:T(8,128)(2,1)}), bf16[128,8,2048]{2,1,0:T(8,128)(2,1)}, u32[]{:S(2)}, u32[]{:S(2)}) async-start(bf16[128,8,2048]{2,1,0:T(8,128)(2,1)} %bitcast.63), calls=%async_computation.3 | async-start | bytes 8388608 | tf_op jit(solution)/shard_map/all_to_all | solution.py:249
  187.1 1.8 select.1
  188.9 0.0 copy-done.11
  188.9 0.0 copy-start.6
  188.9 6.7 %fusion.14 = bf16[1,704,2048]{2,1,0:T(8,128)(2,1)} fusion(bf16[1024,704]{0,1:T(8,128)(2,1)S(1)} %copy-done.11, bf16[1024,2048]{1,0:T(8,128)(2,1)} %bitcast.9), kind=kOutput, calls=%fused_computation.13 | convolution fusion | flops 2954231808 | bytes 8519680 | tf_op jit(solution)/shard_map/dot_general | solution.py:245
  195.6 0.0 copy-done.6
  195.6 0.0 copy-start.9
  195.6 6.7 %fusion.15 = bf16[1,2048,704]{1,2,0:T(8,128)(2,1)} fusion(bf16[1024,704]{0,1:T(8,128)(2,1)S(1)} %copy-done.6, bf16[128,8,2048]{2,1,0:T(8,128)(2,1)} %all-to-all-done), kind=kOutput, calls=%fused_computation.14 | convolution fusion | flops 2954231808 | bytes 8519680 | tf_op jit(solution)/shard_map/dot_general | solution.py:245
  202.3 0.0 copy-done.9
  202.3 6.6 %fusion.18 = bf16[1,2048,704]{1,2,0:T(8,128)(2,1)} fusion(bf16[1024,704]{0,1:T(8,128)(2,1)S(1)} %copy-done.9, bf16[128,8,2048]{2,1,0:T(8,128)(2,1)} %all-to-all-done), kind=kOutput, calls=%fused_computation.15 | convolution fusion | flops 2954231808 | bytes 8519680 | tf_op jit(solution)/shard_map/dot_general | solution.py:245
  209.0 0.0 copy-start.1
  209.0 5.4 %finish_out.1 = (bf16[128,2048]{1,0:T(8,128)(2,1)}, f32[2,128]{1,0:T(2,128)}) custom-call(bf16[128,8,2048]{2,1,0:T(8,128)(2,1)} %all-to-all-done.2.back_ref, bf16[128,1024]{1,0:T(8,128)(2,1)} %get-tuple-element.30.first_ref, bf16[128,1024]{1,0:T(8,128)(2,1)} %get-tuple-element.31.second_ref, f32[2,128]{1,0:T(2,128)} %bitcast.69, bf16[128,2048]{1,0:T(8,128)(2,1)} %cot_ref.3), custom_call_target="tpu_custom_call" | custom-call | flops 1073741824 | bytes 10000000 | tf_op jit(solution)/shard_map/finish_out/pallas_call | solution.py:197
  214.3 24.8 %all-to-all-done.3.back_ref = bf16[128,8,2048]{2,1,0:T(8,128)(2,1)} async-done(((bf16[128,8,2048]{2,1,0:T(8,128)(2,1)}), bf16[128,8,2048]{2,1,0:T(8,128)(2,1)}, u32[]{:S(2)}, u32[]{:S(2)}) %all-to-all-start.3) | async-done | bytes 4194336 | tf_op jit(solution)/shard_map/all_to_all | solution.py:249
  239.1 3.5 %finish_in.1 = bf16[128,2048]{1,0:T(8,128)(2,1)} custom-call(bf16[128,8,2048]{2,1,0:T(8,128)(2,1)} %all-to-all-done.3.back_ref, bf16[128,1024]{1,0:T(8,128)(2,1)} %get-tuple-element.34.both_ref), custom_call_target="tpu_custom_call" | custom-call | tf_op jit(solution)/shard_map/finish_in/pallas_call | solution.py:230
  242.5 0.0 copy-done.1
Async XLA Ops:
  0.6 87.5 %copy-start = (bf16[1,704,2048]{2,1,0:T(8,128)(2,1)S(1)}, bf16[1,704,2048]{2,1,0:T(8,128)(2,1)}, u32[]{:S(2)}) copy-start(bf16[1,704,2048]{2,1,0:T(8,128)(2,1)} %param.15) | copy-start | bytes 8650756
  4.5 63.2 %all-to-all-start = ((bf16[128,8,2048]{2,1,0:T(8,128)(2,1)}), bf16[128,8,2048]{2,1,0:T(8,128)(2,1)}, u32[]{:S(2)}, u32[]{:S(2)}) async-start(bf16[128,8,2048]{2,1,0:T(8,128)(2,1)} %bitcast.62), calls=%async_computation | async-start | bytes 8388608 | tf_op jit(solution)/shard_map/all_to_all | solution.py:249
  67.7 57.1 %all-to-all-start.1 = ((bf16[128,8,2048]{2,1,0:T(8,128)(2,1)}), bf16[128,8,2048]{2,1,0:T(8,128)(2,1)}, u32[]{:S(2)}, u32[]{:S(2)}) async-start(bf16[128,8,2048]{2,1,0:T(8,128)(2,1)} %bitcast.61), calls=%async_computation.1 | async-start | bytes 8388608 | tf_op jit(solution)/shard_map/all_to_all | solution.py:249
  72.9 6.0 %copy-start.3 = (bf16[1,2048,704]{1,2,0:T(8,128)(2,1)S(1)}, bf16[1,2048,704]{1,2,0:T(8,128)(2,1)}, u32[]{:S(2)}) copy-start(bf16[1,2048,704]{1,2,0:T(8,128)(2,1)} %param.14) | copy-start | bytes 8650756
  78.9 8.1 %copy-start.7 = (f32[1024,704]{0,1:T(8,128)}, f32[1024,704]{0,1:T(8,128)S(1)}, u32[]{:S(2)}) copy-start(f32[1024,704]{0,1:T(8,128)S(1)} %fusion.6) | copy-start | bytes 8650756
  87.0 1.1 copy-start.10
  124.8 57.1 %all-to-all-start.2 = ((bf16[128,8,2048]{2,1,0:T(8,128)(2,1)}), bf16[128,8,2048]{2,1,0:T(8,128)(2,1)}, u32[]{:S(2)}, u32[]{:S(2)}) async-start(bf16[128,8,2048]{2,1,0:T(8,128)(2,1)} %bitcast.64), calls=%async_computation.2 | async-start | bytes 8388608 | tf_op jit(solution)/shard_map/all_to_all | solution.py:249
  130.0 7.4 %copy-start.2 = (bf16[1,2048,704]{1,2,0:T(8,128)(2,1)S(1)}, bf16[1,2048,704]{1,2,0:T(8,128)(2,1)}, u32[]{:S(2)}) copy-start(bf16[1,2048,704]{1,2,0:T(8,128)(2,1)} %param.13) | copy-start | bytes 8650756
  137.4 3.6 %copy-start.5 = (bf16[1024,704]{0,1:T(8,128)(2,1)}, bf16[1024,704]{0,1:T(8,128)(2,1)S(1)}, u32[]{:S(2)}) copy-start(bf16[1024,704]{0,1:T(8,128)(2,1)S(1)} %get-tuple-element.37) | copy-start | bytes 4325380
  137.4 3.6 %copy-start.8 = (bf16[1024,704]{0,1:T(8,128)(2,1)}, bf16[1024,704]{0,1:T(8,128)(2,1)S(1)}, u32[]{:S(2)}) copy-start(bf16[1024,704]{0,1:T(8,128)(2,1)S(1)} %get-tuple-element.36) | copy-start | bytes 4325380
  137.5 3.6 %copy-start.4 = (bf16[1,2048,704]{1,2,0:T(8,128)(2,1)S(1)}, bf16[1,2048,704]{1,2,0:T(8,128)(2,1)}, u32[]{:S(2)}) copy-start(bf16[1,2048,704]{1,2,0:T(8,128)(2,1)} %param.14) | copy-start | bytes 8650756
  181.9 7.0 %copy-start.11 = (bf16[1024,704]{0,1:T(8,128)(2,1)S(1)}, bf16[1024,704]{0,1:T(8,128)(2,1)}, u32[]{:S(2)}) copy-start(bf16[1024,704]{0,1:T(8,128)(2,1)} %copy-done.10) | copy-start | bytes 4325380
  181.9 57.1 %all-to-all-start.3 = ((bf16[128,8,2048]{2,1,0:T(8,128)(2,1)}), bf16[128,8,2048]{2,1,0:T(8,128)(2,1)}, u32[]{:S(2)}, u32[]{:S(2)}) async-start(bf16[128,8,2048]{2,1,0:T(8,128)(2,1)} %bitcast.63), calls=%async_computation.3 | async-start | bytes 8388608 | tf_op jit(solution)/shard_map/all_to_all | solution.py:249
  188.9 6.7 %copy-start.6 = (bf16[1024,704]{0,1:T(8,128)(2,1)S(1)}, bf16[1024,704]{0,1:T(8,128)(2,1)}, u32[]{:S(2)}) copy-start(bf16[1024,704]{0,1:T(8,128)(2,1)} %copy-done.5) | copy-start | bytes 4325380
  195.6 6.7 %copy-start.9 = (bf16[1024,704]{0,1:T(8,128)(2,1)S(1)}, bf16[1024,704]{0,1:T(8,128)(2,1)}, u32[]{:S(2)}) copy-start(bf16[1024,704]{0,1:T(8,128)(2,1)} %copy-done.8) | copy-start | bytes 4325380
  209.0 33.6 %copy-start.1 = (bf16[1,704,2048]{2,1,0:T(8,128)(2,1)S(1)}, bf16[1,704,2048]{2,1,0:T(8,128)(2,1)}, u32[]{:S(2)}) copy-start(bf16[1,704,2048]{2,1,0:T(8,128)(2,1)} %param.15) | copy-start | bytes 8650756

commit v5 on v4

--- a/solution.py
+++ b/solution.py
@@ -129,19 +129,21 @@
 def select_kernel(place_ref, first_ref, second_ref, both_ref):
     tokens = place_ref.shape[1]
     rows = first_ref.shape[1]
+    places = [row_to_column(place_ref[j : j + 1, :], tokens) for j in range(2)]
     numbers = lax.broadcasted_iota(jnp.int32, (tokens, rows), 1)
     numbers = (numbers - jnp.where((numbers & CAP) != 0, CAP, 0)).astype(jnp.float32)
-    first = jnp.where(numbers == row_to_column(place_ref[0:1, :], tokens), 1.0, 0.0)
-    second = jnp.where(numbers == row_to_column(place_ref[1:2, :], tokens), 1.0, 0.0)
-    first_ref[...] = first.astype(jnp.bfloat16)
-    second_ref[...] = second.astype(jnp.bfloat16)
-    both_ref[...] = (first + second).astype(jnp.bfloat16)
+    first_ref[...] = jnp.where(numbers == places[0], 1.0, 0.0).astype(jnp.bfloat16)
+    second_ref[...] = jnp.where(numbers == places[1], 1.0, 0.0).astype(jnp.bfloat16)
+    slots = lax.broadcasted_iota(jnp.int32, (tokens, rows // 2), 1)
+    slots = (2 * slots - (slots & (CAP - 1))).astype(jnp.float32)
+    both_ref[...] = jnp.where((slots == places[0]) | (slots == places[1]), 1.0, 0.0).astype(jnp.bfloat16)
 
 
 def select(place):
     tokens = place.shape[1]
     shape = jax.ShapeDtypeStruct((tokens, tokens * CAP), jnp.bfloat16)
-    return pl.pallas_call(select_kernel, out_shape=(shape,) * 3, name="select")(place)
+    half = jax.ShapeDtypeStruct((tokens, tokens * CAP // 2), jnp.bfloat16)
+    return pl.pallas_call(select_kernel, out_shape=(shape, shape, half), name="select")(place)
 
 
 def send_cot_kernel(cot_ref, pick_ref, weight_ref, out_ref):
@@ -219,7 +221,8 @@
 
 
 def finish_in_kernel(back_ref, both_ref, out_ref):
-    rows = back_ref[...].reshape(-1, out_ref.shape[1])
+    rows = (back_ref[:, 0].astype(jnp.float32) + back_ref[:, 1].astype(jnp.float32)).astype(jnp.bfloat16)
+    rows = rows.reshape(-1, out_ref.shape[1])
     out_ref[...] = jnp.dot(both_ref[...], rows, preferred_element_type=jnp.float32).astype(jnp.bfloat16)
 
 
@@ -231,14 +234,14 @@
         finish_in_kernel,
         grid=(steps,),
         in_specs=[
-            pl.BlockSpec((nodes, cap, part), lambda i: (0, 0, i)),
+            pl.BlockSpec((nodes // 2, 2, cap, part), lambda i: (0, 0, 0, i)),
             pl.BlockSpec(both.shape, lambda i: (0, 0)),
         ],
         out_specs=pl.BlockSpec((tokens, part), lambda i: (0, i)),
         out_shape=jax.ShapeDtypeStruct((tokens, width), jnp.bfloat16),
         compiler_params=pltpu.CompilerParams(vmem_limit_bytes=VMEM_LIMIT),
         name="finish_in",
-    )(back, both)
+    )(back.reshape(nodes // 2, 2, cap, width), both)
 
 
 def dot(a, b, a_dim, b_dim):

time: 243 us -> 243 us (level)
  transfers between devices with their start and end apart: 4 -> 4, of which waited for: 4 -> 4; matrix products, arithmetic and copies ran while one was open for 23% -> 23% of each run, Pallas kernels for 6% -> 5%
where the time goes in v5:
time: 243 us; the launch traced here: 242 us
  waiting for transfers between devices  138 us (57%)
  matrix products  55.6 us (23%)
  starting transfers between devices  26.8 us (11%)
  Pallas kernels  20.5 us (8%)
    all_to_all x4, waiting for transfers between devices, exchange(): return lax.all_to_all(rows, AXES, split_axis=0, concat_axis=0, tiled=True)  138 us
    dot_general x9, matrix products, dot(): lax.dot_general(a, b, (((a_dim,), (b_dim,)), ((), ())), preferred_element...  55.6 us
    all_to_all x4, starting transfers between devices, exchange(): return lax.all_to_all(rows, AXES, split_axis=0, concat_axis=0, tiled=True)  26.8 us
    pallas_call x1, Pallas kernels, finish_out(): pl.pallas_call(finish_out_kernel, grid=(steps,), in_specs=[pl.BlockSpec((...  5.35 us
  transfers between devices with their start and end apart: 4, of which 4 were waited for; matrix products, arithmetic and copies ran while one was open for 23% of the time, Pallas kernels for 5%

profile of v5, /device:TPU:7, one launch (start us, length us, event | category | flops | bytes accessed | tf_op | source)
XLA Modules:
  0.0 242.5 jit_solution(3016959612761140297)
XLA Ops:
  0.6 0.0 copy-start
  0.6 3.9 %send_in.1 = bf16[64,2,8,2048]{3,2,1,0:T(8,128)(2,1)} custom-call(bf16[128,2048]{1,0:T(8,128)(2,1)} %coded_hbm.1, f32[16,128]{1,0:T(8,128)} %bitcast.66, s32[2,128]{1,0:T(2,128)} %bitcast.67), custom_call_target="tpu_custom_call" | custom-call | tf_op jit(solution)/shard_map/send_in/pallas_call | solution.py:83
  4.5 11.3 %all-to-all-start = ((bf16[128,8,2048]{2,1,0:T(8,128)(2,1)}), bf16[128,8,2048]{2,1,0:T(8,128)(2,1)}, u32[]{:S(2)}, u32[]{:S(2)}) async-start(bf16[128,8,2048]{2,1,0:T(8,128)(2,1)} %bitcast.63), calls=%async_computation | async-start | bytes 8388608 | tf_op jit(solution)/shard_map/all_to_all | solution.py:252
  15.8 1.7 plan.1
  17.5 4.6 %send_cot.1 = bf16[64,2,8,2048]{3,2,1,0:T(8,128)(2,1)} custom-call(bf16[128,2048]{1,0:T(8,128)(2,1)} %cot_ref.3, bf16[512,128]{1,0:T(8,128)(2,1)} %get-tuple-element.22.pick_ref, f32[512,1]{1,0:T(8,128)} %get-tuple-element.23.weight_ref), custom_call_target="tpu_custom_call" | custom-call | flops 268435456 | bytes 10000000 | tf_op jit(solution)/shard_map/send_cot/pallas_call | solution.py:159
  22.1 45.6 %all-to-all-done = bf16[128,8,2048]{2,1,0:T(8,128)(2,1)} async-done(((bf16[128,8,2048]{2,1,0:T(8,128)(2,1)}), bf16[128,8,2048]{2,1,0:T(8,128)(2,1)}, u32[]{:S(2)}, u32[]{:S(2)}) %all-to-all-start) | async-done | bytes 4194336 | tf_op jit(solution)/shard_map/all_to_all | solution.py:252
  67.7 5.2 %all-to-all-start.1 = ((bf16[128,8,2048]{2,1,0:T(8,128)(2,1)}), bf16[128,8,2048]{2,1,0:T(8,128)(2,1)}, u32[]{:S(2)}, u32[]{:S(2)}) async-start(bf16[128,8,2048]{2,1,0:T(8,128)(2,1)} %bitcast.62), calls=%async_computation.1 | async-start | bytes 8388608 | tf_op jit(solution)/shard_map/all_to_all | solution.py:252
  72.9 0.0 copy-start.3
  72.9 6.0 %fusion.6 = f32[1024,704]{0,1:T(8,128)S(1)} fusion(bf16[128,8,2048]{2,1,0:T(8,128)(2,1)} %all-to-all-done, bf16[1,2048,704]{1,2,0:T(8,128)(2,1)} %param.13), kind=kOutput, calls=%fused_computation.7 | convolution fusion | flops 2952790016 | bytes 9961472 | tf_op jit(solution)/shard_map/dot_general | solution.py:248
  78.9 0.0 copy-done.3
  78.9 0.0 copy-start.7
  78.9 8.1 %multiply_convert_fusion.2 = (bf16[1024,704]{0,1:T(8,128)(2,1)S(1)}, f32[1024,704]{0,1:T(8,128)}) fusion(f32[1024,704]{0,1:T(8,128)S(1)} %fusion.6, bf16[1,2048,704]{1,2,0:T(8,128)(2,1)S(1)} %copy-done.3, bf16[128,8,2048]{2,1,0:T(8,128)(2,1)} %all-to-all-done), kind=kOutput, calls=%fused_computation.26 | convolution fusion | flops 2957115392 | bytes 14286848 | tf_op jit(solution)/shard_map/dot_general | solution.py:248
  87.0 0.0 copy-done.7
  87.0 0.0 copy-start.10
  87.1 1.1 copy-done.10
  88.1 0.0 copy-done
  88.2 5.0 %convolution_convert_fusion = bf16[1024,2048]{1,0:T(8,128)(2,1)} fusion(bf16[1024,704]{0,1:T(8,128)(2,1)S(1)} %get-tuple-element.38, bf16[1,704,2048]{2,1,0:T(8,128)(2,1)S(1)} %copy-done), kind=kOutput, calls=%fused_computation.9 | convolution fusion | flops 2954887168 | bytes 8519680 | tf_op jit(solution)/shard_map/dot_general | solution.py:248
  93.2 31.6 %all-to-all-done.1 = bf16[128,8,2048]{2,1,0:T(8,128)(2,1)} async-done(((bf16[128,8,2048]{2,1,0:T(8,128)(2,1)}), bf16[128,8,2048]{2,1,0:T(8,128)(2,1)}, u32[]{:S(2)}, u32[]{:S(2)}) %all-to-all-start.1) | async-done | bytes 4194336 | tf_op jit(solution)/shard_map/all_to_all | solution.py:252
  124.8 5.2 %all-to-all-start.2 = ((bf16[128,8,2048]{2,1,0:T(8,128)(2,1)}), bf16[128,8,2048]{2,1,0:T(8,128)(2,1)}, u32[]{:S(2)}, u32[]{:S(2)}) async-start(bf16[128,8,2048]{2,1,0:T(8,128)(2,1)} %bitcast.65), calls=%async_computation.2 | async-start | bytes 8388608 | tf_op jit(solution)/shard_map/all_to_all | solution.py:252
  130.0 0.0 copy-start.2
  130.0 7.4 %multiply_convert_fusion = (bf16[1024,704]{0,1:T(8,128)(2,1)S(1)}, bf16[1024,704]{0,1:T(8,128)(2,1)S(1)}) fusion(f32[1024,704]{0,1:T(8,128)} %copy-done.7, f32[1024,704]{0,1:T(8,128)} %get-tuple-element.39, bf16[1024,2048]{1,0:T(8,128)(2,1)} %bitcast.9, bf16[1,704,2048]{2,1,0:T(8,128)(2,1)S(1)} %copy-done), kind=kOutput, calls=%fused_computation.24 | convolution fusion | flops 2962161664 | bytes 15728640 | tf_op jit(solution)/shard_map/dot_general | solution.py:248
  137.4 0.0 copy-start.5
  137.4 0.0 copy-start.8
  137.4 0.0 copy-done.2
  137.5 0.0 copy-start.4
  137.5 3.5 %fusion.26 = f32[1024,2048]{1,0:T(8,128)S(1)} fusion(bf16[1024,704]{0,1:T(8,128)(2,1)S(1)} %get-tuple-element.37, bf16[1,2048,704]{1,2,0:T(8,128)(2,1)S(1)} %copy-done.2), kind=kOutput, calls=%fused_computation.21 | convolution fusion | flops 2952790016 | bytes 12713984 | tf_op jit(solution)/shard_map/dot_general | solution.py:248
  141.0 0.0 copy-done.5
  141.0 0.0 copy-done.8
  141.0 0.0 copy-done.4
  141.0 5.5 %add_convert_fusion = bf16[1024,2048]{1,0:T(8,128)(2,1)} fusion(f32[1024,2048]{1,0:T(8,128)S(1)} %fusion.26, bf16[1024,704]{0,1:T(8,128)(2,1)S(1)} %get-tuple-element.36, bf16[1,2048,704]{1,2,0:T(8,128)(2,1)S(1)} %copy-done.4), kind=kOutput, calls=%fused_computation | convolution fusion | flops 2956984320 | bytes 16908288 | tf_op jit(solution)/shard_map/dot_general | solution.py:248
  146.5 35.4 %all-to-all-done.2.back_ref = bf16[128,8,2048]{2,1,0:T(8,128)(2,1)} async-done(((bf16[128,8,2048]{2,1,0:T(8,128)(2,1)}), bf16[128,8,2048]{2,1,0:T(8,128)(2,1)}, u32[]{:S(2)}, u32[]{:S(2)}) %all-to-all-start.2) | async-done | bytes 4194336 | tf_op jit(solution)/shard_map/all_to_all | solution.py:252
  181.9 0.0 copy-start.11
  181.9 5.2 %all-to-all-start.3 = ((bf16[128,8,2048]{2,1,0:T(8,128)(2,1)}), bf16[128,8,2048]{2,1,0:T(8,128)(2,1)}, u32[]{:S(2)}, u32[]{:S(2)}) async-start(bf16[128,8,2048]{2,1,0:T(8,128)(2,1)} %bitcast.64), calls=%async_computation.3 | async-start | bytes 8388608 | tf_op jit(solution)/shard_map/all_to_all | solution.py:252
  187.1 1.6 select.1
  188.7 0.0 copy-done.11
  188.8 0.0 copy-start.6
  188.8 6.7 %fusion.14 = bf16[1,704,2048]{2,1,0:T(8,128)(2,1)} fusion(bf16[1024,704]{0,1:T(8,128)(2,1)S(1)} %copy-done.11, bf16[1024,2048]{1,0:T(8,128)(2,1)} %bitcast.9), kind=kOutput, calls=%fused_computation.13 | convolution fusion | flops 2954231808 | bytes 8519680 | tf_op jit(solution)/shard_map/dot_general | solution.py:248
  195.5 0.0 copy-done.6
  195.5 0.0 copy-start.9
  195.5 6.7 %fusion.15 = bf16[1,2048,704]{1,2,0:T(8,128)(2,1)} fusion(bf16[1024,704]{0,1:T(8,128)(2,1)S(1)} %copy-done.6, bf16[128,8,2048]{2,1,0:T(8,128)(2,1)} %all-to-all-done), kind=kOutput, calls=%fused_computation.14 | convolution fusion | flops 2954231808 | bytes 8519680 | tf_op jit(solution)/shard_map/dot_general | solution.py:248
  202.2 0.0 copy-done.9
  202.2 6.6 %fusion.18 = bf16[1,2048,704]{1,2,0:T(8,128)(2,1)} fusion(bf16[1024,704]{0,1:T(8,128)(2,1)S(1)} %copy-done.9, bf16[128,8,2048]{2,1,0:T(8,128)(2,1)} %all-to-all-done), kind=kOutput, calls=%fused_computation.15 | convolution fusion | flops 2954231808 | bytes 8519680 | tf_op jit(solution)/shard_map/dot_general | solution.py:248
  208.8 0.0 copy-start.1
  208.8 5.4 %finish_out.1 = (bf16[128,2048]{1,0:T(8,128)(2,1)}, f32[2,128]{1,0:T(2,128)}) custom-call(bf16[128,8,2048]{2,1,0:T(8,128)(2,1)} %all-to-all-done.2.back_ref, bf16[128,1024]{1,0:T(8,128)(2,1)} %get-tuple-element.30.first_ref, bf16[128,1024]{1,0:T(8,128)(2,1)} %get-tuple-element.31.second_ref, f32[2,128]{1,0:T(2,128)} %bitcast.70, bf16[128,2048]{1,0:T(8,128)(2,1)} %cot_ref.3), custom_call_target="tpu_custom_call" | custom-call | flops 1073741824 | bytes 10000000 | tf_op jit(solution)/shard_map/finish_out/pallas_call | solution.py:199
  214.2 24.9 %all-to-all-done.3 = bf16[128,8,2048]{2,1,0:T(8,128)(2,1)} async-done(((bf16[128,8,2048]{2,1,0:T(8,128)(2,1)}), bf16[128,8,2048]{2,1,0:T(8,128)(2,1)}, u32[]{:S(2)}, u32[]{:S(2)}) %all-to-all-start.3) | async-done | bytes 4194336 | tf_op jit(solution)/shard_map/all_to_all | solution.py:252
  239.1 3.4 %finish_in.1 = bf16[128,2048]{1,0:T(8,128)(2,1)} custom-call(bf16[64,2,8,2048]{3,2,1,0:T(8,128)(2,1)} %bitcast.12.back_ref, bf16[128,512]{1,0:T(8,128)(2,1)} %get-tuple-element.34.both_ref), custom_call_target="tpu_custom_call" | custom-call | tf_op jit(solution)/shard_map/finish_in/pallas_call | solution.py:233
  242.5 0.0 copy-done.1
Async XLA Ops:
  0.6 87.5 %copy-start = (bf16[1,704,2048]{2,1,0:T(8,128)(2,1)S(1)}, bf16[1,704,2048]{2,1,0:T(8,128)(2,1)}, u32[]{:S(2)}) copy-start(bf16[1,704,2048]{2,1,0:T(8,128)(2,1)} %param.15) | copy-start | bytes 8650756
  4.5 63.2 %all-to-all-start = ((bf16[128,8,2048]{2,1,0:T(8,128)(2,1)}), bf16[128,8,2048]{2,1,0:T(8,128)(2,1)}, u32[]{:S(2)}, u32[]{:S(2)}) async-start(bf16[128,8,2048]{2,1,0:T(8,128)(2,1)} %bitcast.63), calls=%async_computation | async-start | bytes 8388608 | tf_op jit(solution)/shard_map/all_to_all | solution.py:252
  67.7 57.1 %all-to-all-start.1 = ((bf16[128,8,2048]{2,1,0:T(8,128)(2,1)}), bf16[128,8,2048]{2,1,0:T(8,128)(2,1)}, u32[]{:S(2)}, u32[]{:S(2)}) async-start(bf16[128,8,2048]{2,1,0:T(8,128)(2,1)} %bitcast.62), calls=%async_computation.1 | async-start | bytes 8388608 | tf_op jit(solution)/shard_map/all_to_all | solution.py:252
  72.9 6.0 %copy-start.3 = (bf16[1,2048,704]{1,2,0:T(8,128)(2,1)S(1)}, bf16[1,2048,704]{1,2,0:T(8,128)(2,1)}, u32[]{:S(2)}) copy-start(bf16[1,2048,704]{1,2,0:T(8,128)(2,1)} %param.14) | copy-start | bytes 8650756
  78.9 8.1 %copy-start.7 = (f32[1024,704]{0,1:T(8,128)}, f32[1024,704]{0,1:T(8,128)S(1)}, u32[]{:S(2)}) copy-start(f32[1024,704]{0,1:T(8,128)S(1)} %fusion.6) | copy-start | bytes 8650756
  87.0 1.1 copy-start.10
  124.8 57.1 %all-to-all-start.2 = ((bf16[128,8,2048]{2,1,0:T(8,128)(2,1)}), bf16[128,8,2048]{2,1,0:T(8,128)(2,1)}, u32[]{:S(2)}, u32[]{:S(2)}) async-start(bf16[128,8,2048]{2,1,0:T(8,128)(2,1)} %bitcast.65), calls=%async_computation.2 | async-start | bytes 8388608 | tf_op jit(solution)/shard_map/all_to_all | solution.py:252
  130.0 7.4 %copy-start.2 = (bf16[1,2048,704]{1,2,0:T(8,128)(2,1)S(1)}, bf16[1,2048,704]{1,2,0:T(8,128)(2,1)}, u32[]{:S(2)}) copy-start(bf16[1,2048,704]{1,2,0:T(8,128)(2,1)} %param.13) | copy-start | bytes 8650756
  137.4 3.6 %copy-start.5 = (bf16[1024,704]{0,1:T(8,128)(2,1)}, bf16[1024,704]{0,1:T(8,128)(2,1)S(1)}, u32[]{:S(2)}) copy-start(bf16[1024,704]{0,1:T(8,128)(2,1)S(1)} %get-tuple-element.37) | copy-start | bytes 4325380
  137.4 3.6 %copy-start.8 = (bf16[1024,704]{0,1:T(8,128)(2,1)}, bf16[1024,704]{0,1:T(8,128)(2,1)S(1)}, u32[]{:S(2)}) copy-start(bf16[1024,704]{0,1:T(8,128)(2,1)S(1)} %get-tuple-element.36) | copy-start | bytes 4325380
  137.5 3.6 %copy-start.4 = (bf16[1,2048,704]{1,2,0:T(8,128)(2,1)S(1)}, bf16[1,2048,704]{1,2,0:T(8,128)(2,1)}, u32[]{:S(2)}) copy-start(bf16[1,2048,704]{1,2,0:T(8,128)(2,1)} %param.14) | copy-start | bytes 8650756
  181.9 6.8 %copy-start.11 = (bf16[1024,704]{0,1:T(8,128)(2,1)S(1)}, bf16[1024,704]{0,1:T(8,128)(2,1)}, u32[]{:S(2)}) copy-start(bf16[1024,704]{0,1:T(8,128)(2,1)} %copy-done.10) | copy-start | bytes 4325380
  181.9 57.1 %all-to-all-start.3 = ((bf16[128,8,2048]{2,1,0:T(8,128)(2,1)}), bf16[128,8,2048]{2,1,0:T(8,128)(2,1)}, u32[]{:S(2)}, u32[]{:S(2)}) async-start(bf16[128,8,2048]{2,1,0:T(8,128)(2,1)} %bitcast.64), calls=%async_computation.3 | async-start | bytes 8388608 | tf_op jit(solution)/shard_map/all_to_all | solution.py:252
  188.8 6.7 %copy-start.6 = (bf16[1024,704]{0,1:T(8,128)(2,1)S(1)}, bf16[1024,704]{0,1:T(8,128)(2,1)}, u32[]{:S(2)}) copy-start(bf16[1024,704]{0,1:T(8,128)(2,1)} %copy-done.5) | copy-start | bytes 4325380
  195.5 6.7 %copy-start.9 = (bf16[1024,704]{0,1:T(8,128)(2,1)S(1)}, bf16[1024,704]{0,1:T(8,128)(2,1)}, u32[]{:S(2)}) copy-start(bf16[1024,704]{0,1:T(8,128)(2,1)} %copy-done.8) | copy-start | bytes 4325380
  208.8 33.7 %copy-start.1 = (bf16[1,704,2048]{2,1,0:T(8,128)(2,1)S(1)}, bf16[1,704,2048]{2,1,0:T(8,128)(2,1)}, u32[]{:S(2)}) copy-start(bf16[1,704,2048]{2,1,0:T(8,128)(2,1)} %param.15) | copy-start | bytes 8650756

commit v6 on v4

--- a/solution.py
+++ b/solution.py
@@ -47,7 +47,6 @@
     tokens, width = coded_ref.shape
     blocks = scale_ref.shape[0]
     size = width // blocks
-    part = width // PARTS
     experts = tokens // 2
     copy_routes = pltpu.make_async_copy(routes_hbm, routes_ref, in_sem.at[0])
     copy_routes.start()
@@ -60,16 +59,16 @@
     copy_scale.wait()
     scales = [row_to_column(scale_ref[b : b + 1, :], tokens) for b in range(blocks)]
     copy_coded.wait()
+    for b in range(blocks):
+        columns = pl.ds(b * size, size)
+        coded_ref[:, columns] = (coded_ref[:, columns].astype(jnp.float32) * scales[b]).astype(jnp.bfloat16)
     copies = []
+    deep = experts // PARTS
     for k in range(PARTS):
-        span = pl.ds(k * part, part)
-        for b in range(k * part // size, (k + 1) * part // size):
-            columns = pl.ds(b * size, size)
-            coded_ref[:, columns] = (coded_ref[:, columns].astype(jnp.float32) * scales[b]).astype(jnp.bfloat16)
-        rows = jnp.dot(pick, coded_ref[:, span], preferred_element_type=jnp.float32)
-        rows_ref[:, :, span] = rows.astype(jnp.bfloat16).reshape(experts, CAP, part)
+        rows = jnp.dot(pick[k * deep * CAP : (k + 1) * deep * CAP], coded_ref[...], preferred_element_type=jnp.float32)
+        rows_ref[k * deep : (k + 1) * deep] = rows.astype(jnp.bfloat16).reshape(deep, CAP, width)
         for half in range(2):
-            copy = pltpu.make_async_copy(rows_ref.at[:, :, span], out_hbm.at[:, half, :, span], out_sem.at[k, half])
+            copy = pltpu.make_async_copy(rows_ref.at[pl.ds(k * deep, deep)], out_hbm.at[pl.ds(k * deep, deep), half], out_sem.at[k, half])
             copy.start()
             copies.append(copy)
     for copy in copies:
@@ -257,7 +256,7 @@
 
     send_rows = send_in(coded, block_scale.T, routes.T)
     rows = exchange(send_rows.reshape(nodes, CAP, width))
-    late_routes, _ = lax.optimization_barrier((routes.T, send_rows))
+    late_routes, down_w, _ = lax.optimization_barrier((routes.T, down_w, send_rows))
     pick, slot_weight, place = plan(late_routes, weight)
     rows, send_cots = lax.optimization_barrier((rows, send_cot(cotangent, pick, slot_weight)))
     cot_rows = exchange(send_cots.reshape(nodes, CAP, width))

time: 243 us -> 243 us (level)
  no operation moved by 1% of the time
where the time goes in v6:
time: 243 us
  waiting for transfers between devices  137 us (56%)
  matrix products  55.6 us (23%)
  starting transfers between devices  26.8 us (11%)
  Pallas kernels  20.7 us (9%)
    all_to_all x4, waiting for transfers between devices, exchange(): return lax.all_to_all(rows, AXES, split_axis=0, concat_axis=0, tiled=True)  137 us
    dot_general x9, matrix products, dot(): lax.dot_general(a, b, (((a_dim,), (b_dim,)), ((), ())), preferred_element...  55.6 us
    all_to_all x4, starting transfers between devices, exchange(): return lax.all_to_all(rows, AXES, split_axis=0, concat_axis=0, tiled=True)  26.8 us
    pallas_call x1, Pallas kernels, finish_out(): pl.pallas_call(finish_out_kernel, grid=(steps,), in_specs=[pl.BlockSpec((...  5.35 us
  transfers between devices with their start and end apart: 4, of which 4 were waited for; matrix products, arithmetic and copies ran while one was open for 23% of the time, Pallas kernels for 6%

profile of v6, /device:TPU:7, one launch (start us, length us, event | category | flops | bytes accessed | tf_op | source)
XLA Modules:
  0.0 242.5 jit_solution(2539057511852629187)
XLA Ops:
  0.6 0.0 copy-start
  0.6 3.8 %send_in.1 = bf16[64,2,8,2048]{3,2,1,0:T(8,128)(2,1)} custom-call(bf16[128,2048]{1,0:T(8,128)(2,1)} %coded_hbm.1, f32[16,128]{1,0:T(8,128)} %bitcast.63, s32[2,128]{1,0:T(2,128)} %bitcast.64), custom_call_target="tpu_custom_call" | custom-call | tf_op jit(solution)/shard_map/send_in/pallas_call | solution.py:82
  4.5 11.3 %all-to-all-start = ((bf16[128,8,2048]{2,1,0:T(8,128)(2,1)}), bf16[128,8,2048]{2,1,0:T(8,128)(2,1)}, u32[]{:S(2)}, u32[]{:S(2)}) async-start(bf16[128,8,2048]{2,1,0:T(8,128)(2,1)} %bitcast.60), calls=%async_computation | async-start | bytes 8388608 | tf_op jit(solution)/shard_map/all_to_all | solution.py:248
  15.8 0.0 copy-done
  15.8 1.7 plan.1
  17.5 4.6 %send_cot.1 = bf16[64,2,8,2048]{3,2,1,0:T(8,128)(2,1)} custom-call(bf16[128,2048]{1,0:T(8,128)(2,1)} %cot_ref.3, bf16[512,128]{1,0:T(8,128)(2,1)} %get-tuple-element.23.pick_ref, f32[512,1]{1,0:T(8,128)} %get-tuple-element.24.weight_ref), custom_call_target="tpu_custom_call" | custom-call | flops 268435456 | bytes 10000000 | tf_op jit(solution)/shard_map/send_cot/pallas_call | solution.py:156
  22.0 45.6 %all-to-all-done = bf16[128,8,2048]{2,1,0:T(8,128)(2,1)} async-done(((bf16[128,8,2048]{2,1,0:T(8,128)(2,1)}), bf16[128,8,2048]{2,1,0:T(8,128)(2,1)}, u32[]{:S(2)}, u32[]{:S(2)}) %all-to-all-start) | async-done | bytes 4194336 | tf_op jit(solution)/shard_map/all_to_all | solution.py:248
  67.7 5.2 %all-to-all-start.1 = ((bf16[128,8,2048]{2,1,0:T(8,128)(2,1)}), bf16[128,8,2048]{2,1,0:T(8,128)(2,1)}, u32[]{:S(2)}, u32[]{:S(2)}) async-start(bf16[128,8,2048]{2,1,0:T(8,128)(2,1)} %bitcast.59), calls=%async_computation.1 | async-start | bytes 8388608 | tf_op jit(solution)/shard_map/all_to_all | solution.py:248
  72.9 0.0 copy-start.3
  72.9 6.0 %fusion.6 = f32[1024,704]{0,1:T(8,128)S(1)} fusion(bf16[128,8,2048]{2,1,0:T(8,128)(2,1)} %all-to-all-done, bf16[1,2048,704]{1,2,0:T(8,128)(2,1)} %param.13), kind=kOutput, calls=%fused_computation.7 | convolution fusion | flops 2952790016 | bytes 9961472 | tf_op jit(solution)/shard_map/dot_general | solution.py:244
  78.9 0.0 copy-done.3
  78.9 0.0 copy-start.7
  78.9 8.1 %multiply_convert_fusion.2 = (bf16[1024,704]{0,1:T(8,128)(2,1)S(1)}, f32[1024,704]{0,1:T(8,128)}) fusion(f32[1024,704]{0,1:T(8,128)S(1)} %fusion.6, bf16[1,2048,704]{1,2,0:T(8,128)(2,1)S(1)} %copy-done.3, bf16[128,8,2048]{2,1,0:T(8,128)(2,1)} %all-to-all-done), kind=kOutput, calls=%fused_computation.23 | convolution fusion | flops 2957115392 | bytes 14286848 | tf_op jit(solution)/shard_map/dot_general | solution.py:244
  87.0 0.0 copy-done.7
  87.0 0.0 copy-start.10
  87.0 1.1 copy-done.10
  88.1 5.0 %convolution_convert_fusion = bf16[1024,2048]{1,0:T(8,128)(2,1)} fusion(bf16[1024,704]{0,1:T(8,128)(2,1)S(1)} %get-tuple-element.40, bf16[704,2048]{1,0:T(8,128)(2,1)S(1)} %bitcast.58), kind=kOutput, calls=%fused_computation.9 | convolution fusion | flops 2954887168 | bytes 8519680 | tf_op jit(solution)/shard_map/dot_general | solution.py:244
  93.2 31.6 %all-to-all-done.1 = bf16[128,8,2048]{2,1,0:T(8,128)(2,1)} async-done(((bf16[128,8,2048]{2,1,0:T(8,128)(2,1)}), bf16[128,8,2048]{2,1,0:T(8,128)(2,1)}, u32[]{:S(2)}, u32[]{:S(2)}) %all-to-all-start.1) | async-done | bytes 4194336 | tf_op jit(solution)/shard_map/all_to_all | solution.py:248
  124.8 5.2 %all-to-all-start.2 = ((bf16[128,8,2048]{2,1,0:T(8,128)(2,1)}), bf16[128,8,2048]{2,1,0:T(8,128)(2,1)}, u32[]{:S(2)}, u32[]{:S(2)}) async-start(bf16[128,8,2048]{2,1,0:T(8,128)(2,1)} %bitcast.62), calls=%async_computation.2 | async-start | bytes 8388608 | tf_op jit(solution)/shard_map/all_to_all | solution.py:248
  130.0 0.0 copy-start.2
  130.0 7.4 %multiply_convert_fusion = (bf16[1024,704]{0,1:T(8,128)(2,1)S(1)}, bf16[1024,704]{0,1:T(8,128)(2,1)S(1)}) fusion(f32[1024,704]{0,1:T(8,128)} %copy-done.7, f32[1024,704]{0,1:T(8,128)} %get-tuple-element.41, bf16[1024,2048]{1,0:T(8,128)(2,1)} %bitcast.9, bf16[704,2048]{1,0:T(8,128)(2,1)S(1)} %bitcast.57), kind=kOutput, calls=%fused_computation.21 | convolution fusion | flops 2962161664 | bytes 15728640 | tf_op jit(solution)/shard_map/dot_general | solution.py:244
  137.4 0.0 copy-start.5
  137.4 0.0 copy-start.8
  137.4 0.0 copy-done.2
  137.4 0.0 copy-start.4
  137.4 3.5 %fusion.23 = f32[1024,2048]{1,0:T(8,128)S(1)} fusion(bf16[1024,704]{0,1:T(8,128)(2,1)S(1)} %get-tuple-element.39, bf16[1,2048,704]{1,2,0:T(8,128)(2,1)S(1)} %copy-done.2), kind=kOutput, calls=%fused_computation.18 | convolution fusion | flops 2952790016 | bytes 12713984 | tf_op jit(solution)/shard_map/dot_general | solution.py:244
  141.0 0.0 copy-done.5
  141.0 0.0 copy-done.8
  141.0 0.0 copy-done.4
  141.0 5.5 %add_convert_fusion = bf16[1024,2048]{1,0:T(8,128)(2,1)} fusion(f32[1024,2048]{1,0:T(8,128)S(1)} %fusion.23, bf16[1024,704]{0,1:T(8,128)(2,1)S(1)} %get-tuple-element.38, bf16[1,2048,704]{1,2,0:T(8,128)(2,1)S(1)} %copy-done.4), kind=kOutput, calls=%fused_computation | convolution fusion | flops 2956984320 | bytes 16908288 | tf_op jit(solution)/shard_map/dot_general | solution.py:244
  146.5 35.4 %all-to-all-done.2.back_ref = bf16[128,8,2048]{2,1,0:T(8,128)(2,1)} async-done(((bf16[128,8,2048]{2,1,0:T(8,128)(2,1)}), bf16[128,8,2048]{2,1,0:T(8,128)(2,1)}, u32[]{:S(2)}, u32[]{:S(2)}) %all-to-all-start.2) | async-done | bytes 4194336 | tf_op jit(solution)/shard_map/all_to_all | solution.py:248
  181.9 0.0 copy-start.11
  181.9 5.2 %all-to-all-start.3 = ((bf16[128,8,2048]{2,1,0:T(8,128)(2,1)}), bf16[128,8,2048]{2,1,0:T(8,128)(2,1)}, u32[]{:S(2)}, u32[]{:S(2)}) async-start(bf16[128,8,2048]{2,1,0:T(8,128)(2,1)} %bitcast.61), calls=%async_computation.3 | async-start | bytes 8388608 | tf_op jit(solution)/shard_map/all_to_all | solution.py:248
  187.1 1.8 select.1
  188.9 0.0 copy-done.11
  188.9 0.0 copy-start.6
  188.9 6.7 %fusion.14 = bf16[1,704,2048]{2,1,0:T(8,128)(2,1)} fusion(bf16[1024,704]{0,1:T(8,128)(2,1)S(1)} %copy-done.11, bf16[1024,2048]{1,0:T(8,128)(2,1)} %bitcast.9), kind=kOutput, calls=%fused_computation.13 | convolution fusion | flops 2954231808 | bytes 8519680 | tf_op jit(solution)/shard_map/dot_general | solution.py:244
  195.6 0.0 copy-done.6
  195.6 0.0 copy-start.9
  195.6 6.7 %fusion.15 = bf16[1,2048,704]{1,2,0:T(8,128)(2,1)} fusion(bf16[1024,704]{0,1:T(8,128)(2,1)S(1)} %copy-done.6, bf16[128,8,2048]{2,1,0:T(8,128)(2,1)} %all-to-all-done), kind=kOutput, calls=%fused_computation.14 | convolution fusion | flops 2954231808 | bytes 8519680 | tf_op jit(solution)/shard_map/dot_general | solution.py:244
  202.3 0.0 copy-done.9
  202.3 6.6 %fusion.18 = bf16[1,2048,704]{1,2,0:T(8,128)(2,1)} fusion(bf16[1024,704]{0,1:T(8,128)(2,1)S(1)} %copy-done.9, bf16[128,8,2048]{2,1,0:T(8,128)(2,1)} %all-to-all-done), kind=kOutput, calls=%fused_computation.15 | convolution fusion | flops 2954231808 | bytes 8519680 | tf_op jit(solution)/shard_map/dot_general | solution.py:244
  208.9 0.0 copy-start.1
  208.9 5.4 %finish_out.1 = (bf16[128,2048]{1,0:T(8,128)(2,1)}, f32[2,128]{1,0:T(2,128)}) custom-call(bf16[128,8,2048]{2,1,0:T(8,128)(2,1)} %all-to-all-done.2.back_ref, bf16[128,1024]{1,0:T(8,128)(2,1)} %get-tuple-element.32.first_ref, bf16[128,1024]{1,0:T(8,128)(2,1)} %get-tuple-element.33.second_ref, f32[2,128]{1,0:T(2,128)} %bitcast.67, bf16[128,2048]{1,0:T(8,128)(2,1)} %cot_ref.3), custom_call_target="tpu_custom_call" | custom-call | flops 1073741824 | bytes 10000000 | tf_op jit(solution)/shard_map/finish_out/pallas_call | solution.py:196
  214.3 24.8 %all-to-all-done.3.back_ref = bf16[128,8,2048]{2,1,0:T(8,128)(2,1)} async-done(((bf16[128,8,2048]{2,1,0:T(8,128)(2,1)}), bf16[128,8,2048]{2,1,0:T(8,128)(2,1)}, u32[]{:S(2)}, u32[]{:S(2)}) %all-to-all-start.3) | async-done | bytes 4194336 | tf_op jit(solution)/shard_map/all_to_all | solution.py:248
  239.0 3.5 %finish_in.1 = bf16[128,2048]{1,0:T(8,128)(2,1)} custom-call(bf16[128,8,2048]{2,1,0:T(8,128)(2,1)} %all-to-all-done.3.back_ref, bf16[128,1024]{1,0:T(8,128)(2,1)} %get-tuple-element.36.both_ref), custom_call_target="tpu_custom_call" | custom-call | tf_op jit(solution)/shard_map/finish_in/pallas_call | solution.py:229
  242.5 0.0 copy-done.1
Async XLA Ops:
  0.6 15.1 %copy-start = (bf16[1,704,2048]{2,1,0:T(8,128)(2,1)S(1)}, bf16[1,704,2048]{2,1,0:T(8,128)(2,1)}, u32[]{:S(2)}) copy-start(bf16[1,704,2048]{2,1,0:T(8,128)(2,1)} %param.15) | copy-start | bytes 8650756
  4.5 63.2 %all-to-all-start = ((bf16[128,8,2048]{2,1,0:T(8,128)(2,1)}), bf16[128,8,2048]{2,1,0:T(8,128)(2,1)}, u32[]{:S(2)}, u32[]{:S(2)}) async-start(bf16[128,8,2048]{2,1,0:T(8,128)(2,1)} %bitcast.60), calls=%async_computation | async-start | bytes 8388608 | tf_op jit(solution)/shard_map/all_to_all | solution.py:248
  67.7 57.1 %all-to-all-start.1 = ((bf16[128,8,2048]{2,1,0:T(8,128)(2,1)}), bf16[128,8,2048]{2,1,0:T(8,128)(2,1)}, u32[]{:S(2)}, u32[]{:S(2)}) async-start(bf16[128,8,2048]{2,1,0:T(8,128)(2,1)} %bitcast.59), calls=%async_computation.1 | async-start | bytes 8388608 | tf_op jit(solution)/shard_map/all_to_all | solution.py:248
  72.9 6.0 %copy-start.3 = (bf16[1,2048,704]{1,2,0:T(8,128)(2,1)S(1)}, bf16[1,2048,704]{1,2,0:T(8,128)(2,1)}, u32[]{:S(2)}) copy-start(bf16[1,2048,704]{1,2,0:T(8,128)(2,1)} %param.14) | copy-start | bytes 8650756
  78.9 8.1 %copy-start.7 = (f32[1024,704]{0,1:T(8,128)}, f32[1024,704]{0,1:T(8,128)S(1)}, u32[]{:S(2)}) copy-start(f32[1024,704]{0,1:T(8,128)S(1)} %fusion.6) | copy-start | bytes 8650756
  87.0 1.1 copy-start.10
  124.8 57.1 %all-to-all-start.2 = ((bf16[128,8,2048]{2,1,0:T(8,128)(2,1)}), bf16[128,8,2048]{2,1,0:T(8,128)(2,1)}, u32[]{:S(2)}, u32[]{:S(2)}) async-start(bf16[128,8,2048]{2,1,0:T(8,128)(2,1)} %bitcast.62), calls=%async_computation.2 | async-start | bytes 8388608 | tf_op jit(solution)/shard_map/all_to_all | solution.py:248
  130.0 7.4 %copy-start.2 = (bf16[1,2048,704]{1,2,0:T(8,128)(2,1)S(1)}, bf16[1,2048,704]{1,2,0:T(8,128)(2,1)}, u32[]{:S(2)}) copy-start(bf16[1,2048,704]{1,2,0:T(8,128)(2,1)} %param.13) | copy-start | bytes 8650756
  137.4 3.6 %copy-start.5 = (bf16[1024,704]{0,1:T(8,128)(2,1)}, bf16[1024,704]{0,1:T(8,128)(2,1)S(1)}, u32[]{:S(2)}) copy-start(bf16[1024,704]{0,1:T(8,128)(2,1)S(1)} %get-tuple-element.39) | copy-start | bytes 4325380
  137.4 3.6 %copy-start.8 = (bf16[1024,704]{0,1:T(8,128)(2,1)}, bf16[1024,704]{0,1:T(8,128)(2,1)S(1)}, u32[]{:S(2)}) copy-start(bf16[1024,704]{0,1:T(8,128)(2,1)S(1)} %get-tuple-element.38) | copy-start | bytes 4325380
  137.4 3.6 %copy-start.4 = (bf16[1,2048,704]{1,2,0:T(8,128)(2,1)S(1)}, bf16[1,2048,704]{1,2,0:T(8,128)(2,1)}, u32[]{:S(2)}) copy-start(bf16[1,2048,704]{1,2,0:T(8,128)(2,1)} %param.14) | copy-start | bytes 8650756
  181.9 7.0 %copy-start.11 = (bf16[1024,704]{0,1:T(8,128)(2,1)S(1)}, bf16[1024,704]{0,1:T(8,128)(2,1)}, u32[]{:S(2)}) copy-start(bf16[1024,704]{0,1:T(8,128)(2,1)} %copy-done.10) | copy-start | bytes 4325380
  181.9 57.1 %all-to-all-start.3 = ((bf16[128,8,2048]{2,1,0:T(8,128)(2,1)}), bf16[128,8,2048]{2,1,0:T(8,128)(2,1)}, u32[]{:S(2)}, u32[]{:S(2)}) async-start(bf16[128,8,2048]{2,1,0:T(8,128)(2,1)} %bitcast.61), calls=%async_computation.3 | async-start | bytes 8388608 | tf_op jit(solution)/shard_map/all_to_all | solution.py:248
  188.9 6.7 %copy-start.6 = (bf16[1024,704]{0,1:T(8,128)(2,1)S(1)}, bf16[1024,704]{0,1:T(8,128)(2,1)}, u32[]{:S(2)}) copy-start(bf16[1024,704]{0,1:T(8,128)(2,1)} %copy-done.5) | copy-start | bytes 4325380
  195.6 6.7 %copy-start.9 = (bf16[1024,704]{0,1:T(8,128)(2,1)S(1)}, bf16[1024,704]{0,1:T(8,128)(2,1)}, u32[]{:S(2)}) copy-start(bf16[1024,704]{0,1:T(8,128)(2,1)} %copy-done.8) | copy-start | bytes 4325380
  208.9 33.6 %copy-start.1 = (bf16[1,704,2048]{2,1,0:T(8,128)(2,1)S(1)}, bf16[1,704,2048]{2,1,0:T(8,128)(2,1)}, u32[]{:S(2)}) copy-start(bf16[1,704,2048]{2,1,0:T(8,128)(2,1)} %param.15) | copy-start | bytes 8650756
